TPU v7x, 32 devices: a whole 2x2x4 slice. The times are simulated.
32 devices in a mesh: rep: 2 (over core), fsdp: 16 (over z, y, x).
Axes of the slice: x: 2, y: 2, z: 4, core: 2. Of those that a mesh axis runs over, the one named last changes fastest.
Arguments:
- hidden_in: bfloat16 [4, 1024, 2048], P('rep', 'fsdp'), may hold values from -6 to 6
- cotangent: bfloat16 [4, 1024, 2048], P('rep', 'fsdp'), may hold values from -6 to 6
- lengths: int32 [4], P('rep'), may hold values from 256 to 1024, as said below
- routes: int32 [4, 1024, 6], P('rep', 'fsdp'), may hold values from 0 to 15, all different within a row; in each aligned block of 64 rows (0 to 63, 64 to 127, ..., all dimensions but the last counted through in order) at most 36 rows name the same one
- gate_values: float32 [4, 1024, 6], P('rep', 'fsdp'), may hold values from 0.25 to 1
- attn_gain: bfloat16 [2048], P('fsdp'), may hold values from 0.5 to 1.5
- query_proj: bfloat16 [2048, 3072], P('fsdp'), may hold values from -0.125 to 0.125
- latent_proj: bfloat16 [2048, 576], P('fsdp'), may hold values from -0.125 to 0.125
- latent_gain: bfloat16 [512], P('fsdp'), may hold values from 0.5 to 1.5
- expand_proj: bfloat16 [512, 4096], P('fsdp'), may hold values from -0.25 to 0.25
- output_proj: bfloat16 [2048, 2048], P('fsdp'), may hold values from -1.5 to 1.5
- ffn_gain: bfloat16 [2048], P('fsdp'), may hold values from 0.5 to 1.5
- shared_gate: bfloat16 [2048, 2816], P('fsdp'), may hold values from -0.125 to 0.125
- shared_lift: bfloat16 [2048, 2816], P('fsdp'), may hold values from -0.125 to 0.125
- shared_down: bfloat16 [2816, 2048], P('fsdp'), may hold values from -0.109375 to 0.109375
- expert_gate: bfloat16 [16, 2048, 1408], P('fsdp', None, 'rep'), may hold values from -0.125 to 0.125
- expert_lift: bfloat16 [16, 2048, 1408], P('fsdp', None, 'rep'), may hold values from -0.125 to 0.125
- expert_down: bfloat16 [16, 1408, 2048], P('fsdp', 'rep'), may hold values from -0.15625 to 0.15625
Outputs:
- block_out: bfloat16 [4, 1024, 2048], P('rep', 'fsdp')
- grad_hidden: bfloat16 [4, 1024, 2048], P('rep', 'fsdp')
- grad_attn_gain: float32 [2048], P('fsdp')
- grad_query_proj: float32 [2048, 3072], P('fsdp')
- grad_latent_proj: float32 [2048, 576], P('fsdp')
- grad_latent_gain: float32 [512], P('fsdp')
- grad_expand_proj: float32 [512, 4096], P('fsdp')
- grad_output_proj: float32 [2048, 2048], P('fsdp')
- grad_ffn_gain: float32 [2048], P('fsdp')
- grad_shared_gate: float32 [2048, 2816], P('fsdp')
- grad_shared_lift: float32 [2048, 2816], P('fsdp')
- grad_shared_down: float32 [2816, 2048], P('fsdp')
- grad_expert_gate: float32 [16, 2048, 1408], P('fsdp', None, 'rep')
- grad_expert_lift: float32 [16, 2048, 1408], P('fsdp', None, 'rep')
- grad_expert_down: float32 [16, 1408, 2048], P('fsdp', 'rep')
Inputs may be any that keep to these rules, and one draw needn't show every extreme that they name: `lengths`: in each group of 2 consecutive rows, one row, drawn from the seed, has all 1024 slots used. The 6 routes of a token name different experts. Within each aligned block of 64 positions of a row, no expert is named by more than 36 routes.
All inputs are finite; a program needn't handle non-finite values.
Results may differ from a plain program's by a relative error of at most 0.028.
Values may be sent and summed in bfloat16 or wider, within the bound.
No kernel may reach another device: no remote copies, remote signals or barrier semaphores. Data moves between devices by JAX's collectives and lax.ppermute only.
A program may use at most 512 MiB of HBM per device.

v0:
```python
import jax
import jax.numpy as jnp
from jax import lax
from jax.sharding import PartitionSpec as P

H = 16
DN = 128
DR = 64
DV = 128
R = 512
TOP = 6
MICRO = 2


EPS = 1e-06
THETA = 10000.0
NEG = -1e30


def product(left, right):
    return jnp.dot(left, right, preferred_element_type=jnp.float32)


def contract(form, left, right):
    return jnp.einsum(form, left, right, preferred_element_type=jnp.float32)


def rms_forward(value, gain):
    factor = lax.rsqrt(jnp.mean(value * value, axis=-1, keepdims=True) + EPS)
    return (value * factor * gain, factor)


def rms_backward(value, factor, gain, grad):
    scaled = grad * gain
    inner = jnp.mean(value * scaled, axis=-1, keepdims=True)
    return (
        factor * scaled - value * factor * factor * factor * inner,
        jnp.sum(grad * value * factor, axis=0),
    )


def rope_tables(positions, width):
    half = width // 2
    freqs = THETA ** (-(2.0 * jnp.arange(half, dtype=jnp.float32)) / width)
    angles = positions.astype(jnp.float32)[:, None] * freqs[None, :]
    return (jnp.cos(angles), jnp.sin(angles))


def rotate(value, cosine, sine):
    half = value.shape[-1] // 2
    first = value[..., :half]
    second = value[..., half:]
    return jnp.concatenate(
        [first * cosine - second * sine, second * cosine + first * sine], axis=-1
    )


def rotate_back(grad, cosine, sine):
    half = grad.shape[-1] // 2
    first = grad[..., :half]
    second = grad[..., half:]
    return jnp.concatenate(
        [first * cosine + second * sine, second * cosine - first * sine], axis=-1
    )


def silu_slope(value):
    sigma = jax.nn.sigmoid(value)
    return sigma * (1.0 + value * (1.0 - sigma))


def joined(items):
    return jnp.concatenate(items, axis=0)


def body(
    hidden_in,
    cotangent,
    lengths,
    routes,
    gate_values,
    attn_gain,
    query_proj,
    latent_proj,
    latent_gain,
    expand_proj,
    output_proj,
    ffn_gain,
    shared_gate,
    shared_lift,
    shared_down,
    expert_gate,
    expert_lift,
    expert_down,
):
    tok = hidden_in.shape[1]
    width = hidden_in.shape[2]
    devices = lax.axis_size("fsdp")
    capacity = min(tok, 3 * tok * TOP // (2 * devices))
    seq_len = tok * devices
    scale = (DN + DR) ** (-0.5)
    positions = lax.axis_index("fsdp") * tok + jnp.arange(tok, dtype=jnp.int32)
    key_positions = jnp.arange(seq_len, dtype=jnp.int32)
    cosine, sine = rope_tables(positions, DR)
    head_cos = cosine[:, None, :]
    head_sin = sine[:, None, :]
    slot_ids = jnp.arange(devices * capacity, dtype=jnp.int32)
    expert_ids = jnp.arange(devices, dtype=jnp.int32)
    keep_sh, keep_gl, keep_mx, keep_sg, keep_su = ([], [], [], [], [])
    keep_ho, keep_gr, keep_gq, keep_qn, keep_ol, keep_gh = ([], [], [], [], [], [])
    keep_n1, keep_gqu, keep_gkv = ([], [], [])
    keep_eh, keep_ba, keep_ar, keep_eg, keep_eu = ([], [], [], [], [])
    part_ffn_all, part_latent_all, part_attn_all = ([], [], [])
    outputs = []
    input_grads = []
    fetch_dense = (
        lax.all_gather(attn_gain, "fsdp", axis=0, tiled=True),
        lax.all_gather(query_proj, "fsdp", axis=0, tiled=True),
        lax.all_gather(latent_proj, "fsdp", axis=0, tiled=True),
        lax.all_gather(latent_gain, "fsdp", axis=0, tiled=True),
        lax.all_gather(expand_proj, "fsdp", axis=0, tiled=True),
        lax.all_gather(output_proj, "fsdp", axis=0, tiled=True),
        lax.all_gather(ffn_gain, "fsdp", axis=0, tiled=True),
        lax.all_gather(shared_gate, "fsdp", axis=0, tiled=True),
        lax.all_gather(shared_lift, "fsdp", axis=0, tiled=True),
        lax.all_gather(shared_down, "fsdp", axis=0, tiled=True),
    )
    fetch_experts = (
        lax.all_gather(expert_gate, "rep", axis=2, tiled=True),
        lax.all_gather(expert_lift, "rep", axis=2, tiled=True),
        lax.all_gather(expert_down, "rep", axis=1, tiled=True),
    )
    fetched = (fetch_dense, fetch_experts)
    for step in range(MICRO):
        dense, experts = fetched
        (
            full_attn_gain,
            full_query,
            full_latent,
            full_latent_gain,
            full_expand,
            full_output,
            full_ffn_gain,
            full_share_gate,
            full_share_lift,
            full_share_down,
        ) = dense
        gate_full = experts[0][0]
        lift_full = experts[1][0]
        down_full = experts[2][0]
        length = lengths[step]
        valid_tok = positions < length
        inputs = hidden_in[step].astype(jnp.float32)
        attn_gain_f = full_attn_gain.astype(jnp.float32)
        normed, inv_first = rms_forward(inputs, attn_gain_f)
        normed_low = normed.astype(jnp.bfloat16)
        query = product(normed_low, full_query).reshape(tok, H, DN + DR)
        query_nope = query[:, :, :DN].astype(jnp.bfloat16)
        query_rot = rotate(query[:, :, DN:], head_cos, head_sin).astype(jnp.bfloat16)
        latent_all = product(normed_low, full_latent)
        latent = latent_all[:, :R]
        latent_gain_f = full_latent_gain.astype(jnp.float32)
        latent_norm, inv_latent = rms_forward(latent, latent_gain_f)
        latent_low = latent_norm.astype(jnp.bfloat16)
        key_rot = rotate(latent_all[:, R:], cosine, sine).astype(jnp.bfloat16)
        expand = full_expand.reshape(R, H, DN + DV)
        key_part = expand[:, :, :DN]
        value_part = expand[:, :, DN:]
        query_lat = contract("thd,rhd->thr", query_nope, key_part).astype(jnp.bfloat16)
        latents, rotated = (
            lax.all_gather(latent_low, "fsdp", axis=0, tiled=True),
            lax.all_gather(key_rot, "fsdp", axis=0, tiled=True),
        )
        visible = (key_positions[None, None, :] <= positions[:, None, None]) & (
            key_positions[None, None, :] < length
        )
        scores = scale * (
            contract("thr,sr->ths", query_lat, latents)
            + contract("thd,sd->ths", query_rot, rotated)
        )
        scores = jnp.where(visible, scores, NEG)
        peak = jnp.max(scores, axis=-1, keepdims=True)
        raised = jnp.exp(scores - peak)
        probs = raised / jnp.sum(raised, axis=-1, keepdims=True)
        probs_low = probs.astype(jnp.bfloat16)
        out_lat = contract("ths,sr->thr", probs_low, latents).astype(jnp.bfloat16)
        heads_out = (
            contract("thr,rhd->thd", out_lat, value_part).astype(jnp.bfloat16).reshape(tok, H * DV)
        )
        residual = inputs + product(heads_out, full_output)
        ffn_gain_f = full_ffn_gain.astype(jnp.float32)
        mixed, inv_second = rms_forward(residual, ffn_gain_f)
        mixed_low = mixed.astype(jnp.bfloat16)
        share_gate_v = product(mixed_low, full_share_gate)
        share_lift_v = product(mixed_low, full_share_lift)
        shared_hidden = (jax.nn.silu(share_gate_v) * share_lift_v).astype(jnp.bfloat16)
        shared_out = product(shared_hidden, full_share_down)
        route_flat = routes[step].reshape(tok * TOP)
        hits = (route_flat[:, None] == expert_ids[None, :]).astype(jnp.int32)
        slot = jnp.sum(hits * (jnp.cumsum(hits, axis=0) - 1), axis=1)
        target = route_flat * capacity + slot
        placer = (target[None, :] == slot_ids[:, None]).astype(jnp.bfloat16)
        placer_tok = jnp.sum(placer.reshape(devices * capacity, tok, TOP), axis=2)
        outgoing = (
            product(placer_tok, mixed_low).astype(jnp.bfloat16).reshape(devices, capacity, width)
        )
        arrived = lax.all_to_all(outgoing, "fsdp", split_axis=0, concat_axis=0, tiled=True).reshape(
            devices * capacity, width
        )
        expert_gate_v = product(arrived, gate_full)
        expert_lift_v = product(arrived, lift_full)
        expert_hidden = (jax.nn.silu(expert_gate_v) * expert_lift_v).astype(jnp.bfloat16)
        expert_out = (
            product(expert_hidden, down_full).astype(jnp.bfloat16).reshape(devices, capacity, width)
        )
        returned = lax.all_to_all(
            expert_out, "fsdp", split_axis=0, concat_axis=0, tiled=True
        ).reshape(devices * capacity, width)
        picked = jnp.take(returned, target, axis=0).reshape(tok, TOP, width)
        gate_step = gate_values[step]
        routed_out = jnp.einsum("tk,tkd->td", gate_step, picked.astype(jnp.float32))
        outputs.append((residual + shared_out + routed_out).astype(jnp.bfloat16))
        grad_low = jnp.where(valid_tok[:, None], cotangent[step], jnp.zeros_like(cotangent[step]))
        grad_out = grad_low.astype(jnp.float32)
        keep_sh.append(shared_hidden)
        keep_gl.append(grad_low)
        grad_shared = contract("td,fd->tf", grad_low, full_share_down)
        grad_sg = (grad_shared * share_lift_v * silu_slope(share_gate_v)).astype(jnp.bfloat16)
        grad_su = (grad_shared * jax.nn.silu(share_gate_v)).astype(jnp.bfloat16)
        keep_mx.append(mixed_low)
        keep_sg.append(grad_sg)
        keep_su.append(grad_su)
        grad_mixed = contract("tf,df->td", grad_sg, full_share_gate) + contract(
            "tf,df->td", grad_su, full_share_lift
        )
        route_grad = (
            (gate_step[:, :, None] * grad_out[:, None, :])
            .astype(jnp.bfloat16)
            .reshape(tok * TOP, width)
        )
        back_out = (
            product(placer, route_grad).astype(jnp.bfloat16).reshape(devices, capacity, width)
        )
        back_arrived = lax.all_to_all(
            back_out, "fsdp", split_axis=0, concat_axis=0, tiled=True
        ).reshape(devices * capacity, width)
        keep_eh.append(expert_hidden)
        keep_ba.append(back_arrived)
        grad_eh = contract("cd,fd->cf", back_arrived, down_full)
        grad_eg = (grad_eh * expert_lift_v * silu_slope(expert_gate_v)).astype(jnp.bfloat16)
        grad_eu = (grad_eh * jax.nn.silu(expert_gate_v)).astype(jnp.bfloat16)
        keep_ar.append(arrived)
        keep_eg.append(grad_eg)
        keep_eu.append(grad_eu)
        grad_arrived = contract("cf,df->cd", grad_eg, gate_full) + contract(
            "cf,df->cd", grad_eu, lift_full
        )
        grad_arrived = grad_arrived.astype(jnp.bfloat16).reshape(devices, capacity, width)
        grad_back = lax.all_to_all(
            grad_arrived, "fsdp", split_axis=0, concat_axis=0, tiled=True
        ).reshape(devices * capacity, width)
        grad_mixed = grad_mixed + jnp.sum(
            jnp.take(grad_back, target, axis=0).reshape(tok, TOP, width).astype(jnp.float32), axis=1
        )
        grad_res, part_ffn = rms_backward(residual, inv_second, ffn_gain_f, grad_mixed)
        part_ffn_all.append(part_ffn)
        grad_res = grad_res + grad_out
        grad_res_low = grad_res.astype(jnp.bfloat16)
        keep_ho.append(heads_out)
        keep_gr.append(grad_res_low)
        grad_heads = (
            contract("td,jd->tj", grad_res_low, full_output)
            .astype(jnp.bfloat16)
            .reshape(tok, H, DV)
        )
        keep_ol.append(out_lat)
        keep_gh.append(grad_heads)
        grad_lat = contract("thd,rhd->thr", grad_heads, value_part).astype(jnp.bfloat16)
        grad_probs = contract("thr,sr->ths", grad_lat, latents)
        grad_scores = (
            probs * (grad_probs - jnp.sum(probs * grad_probs, axis=-1, keepdims=True))
        ).astype(jnp.bfloat16)
        grad_qlat = (scale * contract("ths,sr->thr", grad_scores, latents)).astype(jnp.bfloat16)
        grad_qrot = scale * contract("ths,sd->thd", grad_scores, rotated)
        grad_keys_lat = scale * contract("ths,thr->sr", grad_scores, query_lat) + contract(
            "ths,thr->sr", probs_low, grad_lat
        )
        grad_keys_rot = scale * contract("ths,thd->sd", grad_scores, query_rot)
        mine_lat, mine_rot = (
            lax.psum_scatter(
                grad_keys_lat.astype(jnp.bfloat16), "fsdp", scatter_dimension=0, tiled=True
            ).astype(jnp.float32),
            lax.psum_scatter(
                grad_keys_rot.astype(jnp.bfloat16), "fsdp", scatter_dimension=0, tiled=True
            ).astype(jnp.float32),
        )
        keep_gq.append(grad_qlat)
        keep_qn.append(query_nope)
        grad_qnope = contract("thr,rhd->thd", grad_qlat, key_part)
        grad_qrope = rotate_back(grad_qrot, head_cos, head_sin)
        grad_query = (
            jnp.concatenate([grad_qnope, grad_qrope], axis=-1)
            .astype(jnp.bfloat16)
            .reshape(tok, H * (DN + DR))
        )
        keep_n1.append(normed_low)
        keep_gqu.append(grad_query)
        grad_normed = contract("tj,dj->td", grad_query, full_query)
        grad_latent, part_latent = rms_backward(latent, inv_latent, latent_gain_f, mine_lat)
        part_latent_all.append(part_latent)
        grad_krope = rotate_back(mine_rot, cosine, sine)
        grad_kva = jnp.concatenate([grad_latent, grad_krope], axis=-1).astype(jnp.bfloat16)
        keep_gkv.append(grad_kva)
        grad_normed = grad_normed + contract("tj,dj->td", grad_kva, full_latent)
        grad_first, part_attn = rms_backward(inputs, inv_first, attn_gain_f, grad_normed)
        part_attn_all.append(part_attn)
        input_grads.append((grad_first + grad_res).astype(jnp.bfloat16))
    all_n1 = joined(keep_n1)
    all_mx = joined(keep_mx)
    all_ar = joined(keep_ar)
    grad_wk = contract("thr,thd->rhd", joined(keep_gq), joined(keep_qn))
    grad_wv = contract("thr,thd->rhd", joined(keep_ol), joined(keep_gh))
    dense_totals = [
        sum(part_attn_all[1:], part_attn_all[0]),
        contract("td,tj->dj", all_n1, joined(keep_gqu)),
        contract("td,tj->dj", all_n1, joined(keep_gkv)),
        sum(part_latent_all[1:], part_latent_all[0]),
        jnp.concatenate([grad_wk, grad_wv], axis=-1).reshape(R, H * (DN + DV)),
        contract("tj,td->jd", joined(keep_ho), joined(keep_gr)),
        sum(part_ffn_all[1:], part_ffn_all[0]),
        contract("td,tf->df", all_mx, joined(keep_sg)),
        contract("td,tf->df", all_mx, joined(keep_su)),
        contract("tf,td->fd", joined(keep_sh), joined(keep_gl)),
    ]
    expert_totals = [
        contract("cd,cf->df", all_ar, joined(keep_eg))[None],
        contract("cd,cf->df", all_ar, joined(keep_eu))[None],
        contract("cf,cd->fd", joined(keep_eh), joined(keep_ba))[None],
    ]
    dense_sums = (
        lax.psum_scatter(
            dense_totals[0].astype(jnp.bfloat16), "fsdp", scatter_dimension=0, tiled=True
        ).astype(jnp.float32),
        lax.psum_scatter(
            dense_totals[1].astype(jnp.bfloat16), "fsdp", scatter_dimension=0, tiled=True
        ).astype(jnp.float32),
        lax.psum_scatter(
            dense_totals[2].astype(jnp.bfloat16), "fsdp", scatter_dimension=0, tiled=True
        ).astype(jnp.float32),
        lax.psum_scatter(
            dense_totals[3].astype(jnp.bfloat16), "fsdp", scatter_dimension=0, tiled=True
        ).astype(jnp.float32),
        lax.psum_scatter(
            dense_totals[4].astype(jnp.bfloat16), "fsdp", scatter_dimension=0, tiled=True
        ).astype(jnp.float32),
        lax.psum_scatter(
            dense_totals[5].astype(jnp.bfloat16), "fsdp", scatter_dimension=0, tiled=True
        ).astype(jnp.float32),
        lax.psum_scatter(
            dense_totals[6].astype(jnp.bfloat16), "fsdp", scatter_dimension=0, tiled=True
        ).astype(jnp.float32),
        lax.psum_scatter(
            dense_totals[7].astype(jnp.bfloat16), "fsdp", scatter_dimension=0, tiled=True
        ).astype(jnp.float32),
        lax.psum_scatter(
            dense_totals[8].astype(jnp.bfloat16), "fsdp", scatter_dimension=0, tiled=True
        ).astype(jnp.float32),
        lax.psum_scatter(
            dense_totals[9].astype(jnp.bfloat16), "fsdp", scatter_dimension=0, tiled=True
        ).astype(jnp.float32),
    )
    dense_sums = (
        lax.psum(dense_sums[0].astype(jnp.bfloat16), "rep").astype(jnp.float32),
        lax.psum(dense_sums[1].astype(jnp.bfloat16), "rep").astype(jnp.float32),
        lax.psum(dense_sums[2].astype(jnp.bfloat16), "rep").astype(jnp.float32),
        lax.psum(dense_sums[3].astype(jnp.bfloat16), "rep").astype(jnp.float32),
        lax.psum(dense_sums[4].astype(jnp.bfloat16), "rep").astype(jnp.float32),
        lax.psum(dense_sums[5].astype(jnp.bfloat16), "rep").astype(jnp.float32),
        lax.psum(dense_sums[6].astype(jnp.bfloat16), "rep").astype(jnp.float32),
        lax.psum(dense_sums[7].astype(jnp.bfloat16), "rep").astype(jnp.float32),
        lax.psum(dense_sums[8].astype(jnp.bfloat16), "rep").astype(jnp.float32),
        lax.psum(dense_sums[9].astype(jnp.bfloat16), "rep").astype(jnp.float32),
    )
    expert_sums = (
        lax.psum_scatter(
            expert_totals[0].astype(jnp.bfloat16), "rep", scatter_dimension=2, tiled=True
        ).astype(jnp.float32),
        lax.psum_scatter(
            expert_totals[1].astype(jnp.bfloat16), "rep", scatter_dimension=2, tiled=True
        ).astype(jnp.float32),
        lax.psum_scatter(
            expert_totals[2].astype(jnp.bfloat16), "rep", scatter_dimension=1, tiled=True
        ).astype(jnp.float32),
    )
    return (
        jnp.stack(outputs),
        jnp.stack(input_grads),
        dense_sums[0],
        dense_sums[1],
        dense_sums[2],
        dense_sums[3],
        dense_sums[4],
        dense_sums[5],
        dense_sums[6],
        dense_sums[7],
        dense_sums[8],
        dense_sums[9],
        expert_sums[0],
        expert_sums[1],
        expert_sums[2],
    )


def solution(mesh):
    in_specs = (
        P("rep", "fsdp", None),
        P("rep", "fsdp", None),
        P("rep"),
        P("rep", "fsdp", None),
        P("rep", "fsdp", None),
        P("fsdp"),
        P("fsdp", None),
        P("fsdp", None),
        P("fsdp"),
        P("fsdp", None),
        P("fsdp", None),
        P("fsdp"),
        P("fsdp", None),
        P("fsdp", None),
        P("fsdp", None),
        P("fsdp", None, "rep"),
        P("fsdp", None, "rep"),
        P("fsdp", "rep", None),
    )
    out_specs = (
        P("rep", "fsdp", None),
        P("rep", "fsdp", None),
        P("fsdp"),
        P("fsdp", None),
        P("fsdp", None),
        P("fsdp"),
        P("fsdp", None),
        P("fsdp", None),
        P("fsdp"),
        P("fsdp", None),
        P("fsdp", None),
        P("fsdp", None),
        P("fsdp", None, "rep"),
        P("fsdp", None, "rep"),
        P("fsdp", "rep", None),
    )
    return jax.shard_map(body, mesh=mesh, in_specs=in_specs, out_specs=out_specs, check_vma=False)
```

profile of v0, /device:TPU:0, one launch (start us, length us, event | category | flops | bytes accessed | tf_op | source)
XLA Modules:
  0.0 3213.1 jit_solution(3992359351590430258)
XLA Ops:
  12.3 43.7 %all-reduce = bf16[512]{0:T(512)(128)(2,1)S(1)} all-reduce(bf16[512]{0:T(512)(128)(2,1)S(1)} %dynamic-update-slice), channel_id=1, replica_groups=mesh['rep'=2,'fsdp'=16] {'fsdp'}, use_global_device_ids=true, to_apply=%add | all-reduce | flops 512 | bytes 2048
  56.0 35.6 %all-gather = bf16[16,1,128]{2,1,0:T(2,128)(2,1)S(1)} all-gather(bf16[1,1,128]{2,1,0:T(2,128)(2,1)} %bitcast.430), channel_id=1, replica_groups=mesh['rep'=2,'fsdp'=16] {'fsdp'}, dimensions={0}, use_global_device_ids=true | all-gather | bytes 4352 | tf_op jit(solution)/shard_map/all_gather | solution.py:117
  127.8 89.7 %all-gather.1 = bf16[16,1,128]{2,1,0:T(2,128)(2,1)S(1)} all-gather(bf16[1,1,128]{2,1,0:T(2,128)(2,1)S(1)} %bitcast.431), channel_id=1, replica_groups=mesh['rep'=2,'fsdp'=16] {'fsdp'}, dimensions={0}, use_global_device_ids=true | all-gather | bytes 4352 | tf_op jit(solution)/shard_map/all_gather | solution.py:123
  223.3 45.8 %all_gather.57 = bf16[1024,64]{1,0:T(8,128)(2,1)S(1)} all-gather(bf16[64,64]{1,0:T(8,128)(2,1)S(1)} %pad_maximum_fusion.15), channel_id=1, replica_groups=mesh['rep'=2,'fsdp'=16] {'fsdp'}, dimensions={0}, use_global_device_ids=true | all-gather | bytes 139264 | tf_op jit(solution)/shard_map/all_gather | solution.py:172
  275.6 75.9 %all-gather.15.cloned.1.call-done = bf16[2048,3072]{1,0:T(8,128)(2,1)} async-done(((bf16[128,3072]{1,0:T(8,128)(2,1)}), bf16[2048,3072]{1,0:T(8,128)(2,1)}) %all-gather.15.cloned.1.call-update) | async-done | bytes 12582928 | tf_op jit(solution)/shard_map/all_gather | solution.py:118
  351.5 16.8 copy.168
  368.3 8.9 fusion.220
  381.1 27.1 all-gather.21.cloned.1.call-done
  420.0 102.5 %all-gather.23.cloned.1.call-done = bf16[2048,2048]{1,0:T(8,128)(2,1)} async-done(((bf16[128,2048]{1,0:T(8,128)(2,1)}), bf16[2048,2048]{1,0:T(8,128)(2,1)}) %all-gather.23.cloned.1.call-update) | async-done | bytes 8388624 | tf_op jit(solution)/shard_map/all_gather | solution.py:122
  543.3 8.9 fusion.7
  552.2 38.7 %all-to-all-done = bf16[16,36,2048]{2,1,0:T(8,128)(2,1)} async-done(((bf16[16,36,2048]{2,1,0:T(8,128)(2,1)}), bf16[16,36,2048]{2,1,0:T(8,128)(2,1)}, u32[]{:S(2)}, u32[]{:S(2)}) %all-to-all-start) | async-done | bytes 2359328 | tf_op jit(solution)/shard_map/all_to_all | solution.py:207
  595.0 8.9 fusion.19
  603.9 11.4 multiply_convert_fusion.5
  629.0 27.4 all-to-all-start.1
  674.3 70.6 %all-to-all-done.1 = bf16[16,36,2048]{2,1,0:T(8,128)(2,1)} async-done(((bf16[16,36,2048]{2,1,0:T(8,128)(2,1)}), bf16[16,36,2048]{2,1,0:T(8,128)(2,1)}, u32[]{:S(2)}, u32[]{:S(2)}) %all-to-all-start.1) | async-done | bytes 2359328 | tf_op jit(solution)/shard_map/all_to_all | solution.py:216
  745.0 30.6 all-to-all-start.5
  782.0 170.5 %all-gather.25.cloned.1.call-done = bf16[2048,2816]{1,0:T(8,128)(2,1)} async-done(((bf16[128,2816]{1,0:T(8,128)(2,1)}), bf16[2048,2816]{1,0:T(8,128)(2,1)}) %all-gather.25.cloned.1.call-update) | async-done | bytes 11534352 | tf_op jit(solution)/shard_map/all_gather | solution.py:124
  958.9 136.8 %all-gather.29.cloned.1.call-done = bf16[2816,2048]{1,0:T(8,128)(2,1)} async-done(((bf16[176,2048]{1,0:T(8,128)(2,1)}), bf16[2816,2048]{1,0:T(8,128)(2,1)}) %all-gather.29.cloned.1.call-update) | async-done | bytes 11534352 | tf_op jit(solution)/shard_map/all_gather | solution.py:126
  1095.7 8.9 multiply_convert_fusion.16
  1179.6 85.7 %all_gather.67 = bf16[1024,64]{1,0:T(8,128)(2,1)S(1)} all-gather(bf16[64,64]{1,0:T(8,128)(2,1)S(1)} %pad_maximum_fusion.16), channel_id=1, replica_groups=mesh['rep'=2,'fsdp'=16] {'fsdp'}, dimensions={0}, use_global_device_ids=true | all-gather | bytes 139264 | tf_op jit(solution)/shard_map/all_gather | solution.py:172
  1285.0 43.8 %all-gather.37.cloned.1.call-done = bf16[1024,512]{1,0:T(8,128)(2,1)} async-done(((bf16[64,512]{1,0:T(8,128)(2,1)}), bf16[1024,512]{1,0:T(8,128)(2,1)}) %all-gather.37.cloned.1.call-update) | async-done | bytes 1048592 | tf_op jit(solution)/shard_map/all_gather | solution.py:171
  1356.3 9.0 fusion.5
  1365.4 39.6 %all-to-all-done.2 = bf16[16,36,2048]{2,1,0:T(8,128)(2,1)} async-done(((bf16[16,36,2048]{2,1,0:T(8,128)(2,1)}), bf16[16,36,2048]{2,1,0:T(8,128)(2,1)}, u32[]{:S(2)}, u32[]{:S(2)}) %all-to-all-start.2) | async-done | bytes 2359328 | tf_op jit(solution)/shard_map/all_to_all | solution.py:207
  1407.7 9.0 fusion.17
  1416.7 9.8 multiply_convert_fusion.3
  1436.8 11.9 all-to-all-start.7
  1457.8 42.3 %all-to-all-done.7 = bf16[16,36,2048]{2,1,0:T(8,128)(2,1)} async-done(((bf16[16,36,2048]{2,1,0:T(8,128)(2,1)}), bf16[16,36,2048]{2,1,0:T(8,128)(2,1)}, u32[]{:S(2)}, u32[]{:S(2)}) %all-to-all-start.7) | async-done | bytes 2359328 | tf_op jit(solution)/shard_map/all_to_all | solution.py:259
  1500.2 12.0 all-to-all-start.3
  1546.6 18.3 all-to-all-done.3
  1618.8 76.6 %reduce-scatter.27.cloned.1.call-done = bf16[64,64]{1,0:T(8,128)(2,1)} async-done(((bf16[1024,64]{1,0:T(8,128)(2,1)}), bf16[64,64]{1,0:T(8,128)(2,1)}) %reduce-scatter.27.cloned.1.call-update) | async-done | bytes 8208 | tf_op jit(solution)/shard_map/reduce_scatter | solution.py:293
  1696.4 76.0 %reduce-scatter.25.cloned.1.call-done = bf16[64,512]{1,0:T(8,128)(2,1)} async-done(((bf16[1024,512]{1,0:T(8,128)(2,1)}), bf16[64,512]{1,0:T(8,128)(2,1)}) %reduce-scatter.25.cloned.1.call-update) | async-done | bytes 65552 | tf_op jit(solution)/shard_map/reduce_scatter | solution.py:290
  1854.7 10.8 fusion.3
  1865.5 27.9 copy.227
  1893.4 10.6 copy.323
  1905.9 12.8 fusion.2
  1918.8 28.0 copy.225
  1946.7 10.5 copy.324
  1958.9 12.3 fusion.4
  1983.0 9.4 fusion.362
  2004.0 9.4 fusion.364
  2015.2 180.1 %reduce-scatter.39.cloned.1.call-done = bf16[176,2048]{1,0:T(8,128)(2,1)} async-done(((bf16[2816,2048]{1,0:T(8,128)(2,1)}), bf16[176,2048]{1,0:T(8,128)(2,1)}) %reduce-scatter.39.cloned.1.call-update) | async-done | bytes 720912 | tf_op jit(solution)/shard_map/reduce_scatter | solution.py:368
  2195.3 247.7 %reduce-scatter.37.cloned.1.call-done = bf16[128,2816]{1,0:T(8,128)(2,1)} async-done(((bf16[2048,2816]{1,0:T(8,128)(2,1)}), bf16[128,2816]{1,0:T(8,128)(2,1)}) %reduce-scatter.37.cloned.1.call-update) | async-done | bytes 720912 | tf_op jit(solution)/shard_map/reduce_scatter | solution.py:365
  2443.1 247.9 %reduce-scatter.35.cloned.1.call-done = bf16[128,2816]{1,0:T(8,128)(2,1)} async-done(((bf16[2048,2816]{1,0:T(8,128)(2,1)}), bf16[128,2816]{1,0:T(8,128)(2,1)}) %reduce-scatter.35.cloned.1.call-update) | async-done | bytes 720912 | tf_op jit(solution)/shard_map/reduce_scatter | solution.py:362
  2691.0 184.8 %reduce-scatter.33.cloned.1.call-done = bf16[128,2048]{1,0:T(8,128)(2,1)} async-done(((bf16[2048,2048]{1,0:T(8,128)(2,1)}), bf16[128,2048]{1,0:T(8,128)(2,1)}) %reduce-scatter.33.cloned.1.call-update) | async-done | bytes 524304 | tf_op jit(solution)/shard_map/reduce_scatter | solution.py:356
  2875.8 212.1 %reduce-scatter.29.cloned.1.call-done = bf16[128,3072]{1,0:T(8,128)(2,1)} async-done(((bf16[2048,3072]{1,0:T(8,128)(2,1)}), bf16[128,3072]{1,0:T(8,128)(2,1)}) %reduce-scatter.29.cloned.1.call-update) | async-done | bytes 786448 | tf_op jit(solution)/shard_map/reduce_scatter | solution.py:344
  3092.1 41.7 %all-reduce.4 = (bf16[2048]{0:T(1024)(128)(2,1)S(1)}, bf16[512]{0:T(512)(128)(2,1)S(1)}, bf16[2048]{0:T(1024)(128)(2,1)S(1)}) all-reduce(bf16[2048]{0:T(1024)(128)(2,1)S(1)} %add_convert_fusion.7, bf16[512]{0:T(512)(128)(2,1)S(1)} %copy-done.164, bf16[2048]{0:T(1024)(128)(2,1)S(1)} %copy-done.143), channel_id=6, replica_groups=mesh['rep'=2,'fsdp'=16] {'fsdp'}, use_global_device_ids=true, to_apply=%region_34.36.clone | all-reduce | flops 4608 | bytes 18432
  3149.5 13.5 copy.228
  3173.5 13.2 copy.226
  (704 shorter events, 528.2 us)
Async XLA Ops:
  7.2 87.6 %all-gather.19.cloned.1.call-start = ((), (), s32[]{:S(2)}) async-start(), calls=%async_computation.24 | async-start | bytes 2506752 | tf_op jit(solution)/shard_map/all_gather | solution.py:119
  7.9 261.2 %all-gather.17.cloned.1.call-start = ((), (), s32[]{:S(2)}) async-start(), calls=%async_computation.23 | async-start | bytes 4456448 | tf_op jit(solution)/shard_map/all_gather | solution.py:121
  8.7 342.8 %all-gather.15.cloned.1.call-start = ((), (), s32[]{:S(2)}) async-start(), calls=%async_computation.22 | async-start | bytes 13369344 | tf_op jit(solution)/shard_map/all_gather | solution.py:118
  9.4 398.8 %all-gather.21.cloned.1.call-start = ((), (), s32[]{:S(2)}) async-start(), calls=%async_computation.25 | async-start | bytes 1114112 | tf_op jit(solution)/shard_map/all_gather | solution.py:171
  91.6 276.6 %copy-start.117 = (f32[16,1,128]{2,1,0:T(1,128)}, f32[16,1,128]{2,1,0:T(1,128)S(1)}, u32[]{:S(2)}) copy-start(f32[16,1,128]{2,1,0:T(1,128)S(1)} %convert_element_type.540) | copy-start | bytes 24580
  92.9 275.4 %copy-start.145 = (f32[64]{0:T(128)}, f32[64]{0:T(128)S(1)}, u32[]{:S(2)}) copy-start(f32[64]{0:T(128)S(1)} %get-tuple-element.181) | copy-start | bytes 772
  98.8 423.7 %all-gather.23.cloned.1.call-start = ((), (), s32[]{:S(2)}) async-start(), calls=%async_computation.26 | async-start | bytes 8912896 | tf_op jit(solution)/shard_map/all_gather | solution.py:122
  99.4 443.9 %all-gather.35.cloned.1.call-start = ((), (), s32[]{:S(2)}) async-start(), calls=%async_computation.32 | async-start | bytes 8650752 | tf_op jit(solution)/shard_map/all_gather | solution.py:131
  100.0 495.0 %all-gather.33.cloned.1.call-start = ((), (), s32[]{:S(2)}) async-start(), calls=%async_computation.31 | async-start | bytes 8650752 | tf_op jit(solution)/shard_map/all_gather | solution.py:130
  100.8 503.1 %all-gather.31.cloned.1.call-start = ((), (), s32[]{:S(2)}) async-start(), calls=%async_computation.30 | async-start | bytes 8650752 | tf_op jit(solution)/shard_map/all_gather | solution.py:129
  101.5 674.2 %all-gather.27.cloned.1.call-start = ((), (), s32[]{:S(2)}) async-start(), calls=%async_computation.28 | async-start | bytes 12255232 | tf_op jit(solution)/shard_map/all_gather | solution.py:125
  102.3 850.3 %all-gather.25.cloned.1.call-start = ((), (), s32[]{:S(2)}) async-start(), calls=%async_computation.27 | async-start | bytes 12255232 | tf_op jit(solution)/shard_map/all_gather | solution.py:124
  107.9 1034.8 %copy-start.17 = (bf16[64,2048]{1,0:T(8,128)(2,1)}, bf16[64,2048]{1,0:T(8,128)(2,1)S(1)}, u32[]{:S(2)}) copy-start(bf16[64,2048]{1,0:T(8,128)(2,1)S(1)} %get-tuple-element.131) | copy-start | bytes 786436
  120.6 413.7 %all-to-all-start.4 = ((bf16[16,36,2048]{2,1,0:T(8,128)(2,1)}), bf16[16,36,2048]{2,1,0:T(8,128)(2,1)}, u32[]{:S(2)}, u32[]{:S(2)}) async-start(bf16[16,36,2048]{2,1,0:T(8,128)(2,1)} %reshape.526), calls=%async_computation.4 | async-start | bytes 5242880 | tf_op jit(solution)/shard_map/all_to_all | solution.py:244
  125.3 970.4 %all-gather.29.cloned.1.call-start = ((), (), s32[]{:S(2)}) async-start(), calls=%async_computation.29 | async-start | bytes 12255232 | tf_op jit(solution)/shard_map/all_gather | solution.py:126
  217.5 1374.8 %copy-start.103 = (f32[16,1,128]{2,1,0:T(1,128)}, f32[16,1,128]{2,1,0:T(1,128)S(1)}, u32[]{:S(2)}) copy-start(f32[16,1,128]{2,1,0:T(1,128)S(1)} %convert_element_type.541) | copy-start | bytes 24580
  527.6 615.2 %copy-start.8 = (f32[64,2048]{1,0:T(8,128)}, f32[64,2048]{1,0:T(8,128)S(1)}, u32[]{:S(2)}) copy-start(f32[64,2048]{1,0:T(8,128)S(1)} %get-tuple-element.168) | copy-start | bytes 1572868
  527.6 615.1 %copy-start.154 = (f32[64]{0:T(128)}, f32[64]{0:T(128)S(1)}, u32[]{:S(2)}) copy-start(f32[64]{0:T(128)S(1)} %add_rsqrt_fusion.3) | copy-start | bytes 772
  527.7 424.8 %copy-start.15 = (bf16[64,2048]{1,0:T(8,128)(2,1)}, bf16[64,2048]{1,0:T(8,128)(2,1)S(1)}, u32[]{:S(2)}) copy-start(bf16[64,2048]{1,0:T(8,128)(2,1)S(1)} %multiply_convert_fusion.21) | copy-start | bytes 786436
  534.3 56.6 %all-to-all-start = ((bf16[16,36,2048]{2,1,0:T(8,128)(2,1)}), bf16[16,36,2048]{2,1,0:T(8,128)(2,1)}, u32[]{:S(2)}, u32[]{:S(2)}) async-start(bf16[16,36,2048]{2,1,0:T(8,128)(2,1)} %reshape.514), calls=%async_computation | async-start | bytes 5242880 | tf_op jit(solution)/shard_map/all_to_all | solution.py:207
  629.0 116.0 %all-to-all-start.1 = ((bf16[16,36,2048]{2,1,0:T(8,128)(2,1)}), bf16[16,36,2048]{2,1,0:T(8,128)(2,1)}, u32[]{:S(2)}, u32[]{:S(2)}) async-start(bf16[16,36,2048]{2,1,0:T(8,128)(2,1)} %reshape.516), calls=%async_computation.1 | async-start | bytes 5242880 | tf_op jit(solution)/shard_map/all_to_all | solution.py:216
  745.0 370.4 %all-to-all-start.5 = ((bf16[16,36,2048]{2,1,0:T(8,128)(2,1)}), bf16[16,36,2048]{2,1,0:T(8,128)(2,1)}, u32[]{:S(2)}, u32[]{:S(2)}) async-start(bf16[16,36,2048]{2,1,0:T(8,128)(2,1)} %reshape.528), calls=%async_computation.5 | async-start | bytes 5242880 | tf_op jit(solution)/shard_map/all_to_all | solution.py:259
  775.6 489.8 %reduce-scatter.21.cloned.1.call-start = ((), (), s32[]{:S(2)}) async-start(), calls=%async_computation.34 | async-start | bytes 1114112 | tf_op jit(solution)/shard_map/reduce_scatter | solution.py:290
  1174.6 174.1 %all-to-all-start.6 = ((bf16[16,36,2048]{2,1,0:T(8,128)(2,1)}), bf16[16,36,2048]{2,1,0:T(8,128)(2,1)}, u32[]{:S(2)}, u32[]{:S(2)}) async-start(bf16[16,36,2048]{2,1,0:T(8,128)(2,1)} %reshape.531), calls=%async_computation.8 | async-start | bytes 5242880 | tf_op jit(solution)/shard_map/all_to_all | solution.py:244
  1179.2 149.6 %all-gather.37.cloned.1.call-start = ((), (), s32[]{:S(2)}) async-start(), calls=%async_computation.33 | async-start | bytes 1114112 | tf_op jit(solution)/shard_map/all_gather | solution.py:171
  1345.6 246.7 %copy-start.10 = (f32[64,2048]{1,0:T(8,128)}, f32[64,2048]{1,0:T(8,128)S(1)}, u32[]{:S(2)}) copy-start(f32[64,2048]{1,0:T(8,128)S(1)} %get-tuple-element.175) | copy-start | bytes 1572868
  1345.7 246.7 %copy-start.156 = (f32[64]{0:T(128)}, f32[64]{0:T(128)S(1)}, u32[]{:S(2)}) copy-start(f32[64]{0:T(128)S(1)} %add_rsqrt_fusion) | copy-start | bytes 772
  1348.8 56.2 %all-to-all-start.2 = ((bf16[16,36,2048]{2,1,0:T(8,128)(2,1)}), bf16[16,36,2048]{2,1,0:T(8,128)(2,1)}, u32[]{:S(2)}, u32[]{:S(2)}) async-start(bf16[16,36,2048]{2,1,0:T(8,128)(2,1)} %reshape.521), calls=%async_computation.2 | async-start | bytes 5242880 | tf_op jit(solution)/shard_map/all_to_all | solution.py:207
  1436.8 63.4 %all-to-all-start.7 = ((bf16[16,36,2048]{2,1,0:T(8,128)(2,1)}), bf16[16,36,2048]{2,1,0:T(8,128)(2,1)}, u32[]{:S(2)}, u32[]{:S(2)}) async-start(bf16[16,36,2048]{2,1,0:T(8,128)(2,1)} %reshape.533), calls=%async_computation.9 | async-start | bytes 5242880 | tf_op jit(solution)/shard_map/all_to_all | solution.py:259
  1500.2 64.7 %all-to-all-start.3 = ((bf16[16,36,2048]{2,1,0:T(8,128)(2,1)}), bf16[16,36,2048]{2,1,0:T(8,128)(2,1)}, u32[]{:S(2)}, u32[]{:S(2)}) async-start(bf16[16,36,2048]{2,1,0:T(8,128)(2,1)} %reshape.523), calls=%async_computation.3 | async-start | bytes 5242880 | tf_op jit(solution)/shard_map/all_to_all | solution.py:216
  1512.2 105.9 %reduce-scatter.23.cloned.1.call-start = ((), (), s32[]{:S(2)}) async-start(), calls=%async_computation.35 | async-start | bytes 278528 | tf_op jit(solution)/shard_map/reduce_scatter | solution.py:293
  1513.8 181.6 %reduce-scatter.27.cloned.1.call-start = ((), (), s32[]{:S(2)}) async-start(), calls=%async_computation.37 | async-start | bytes 278528 | tf_op jit(solution)/shard_map/reduce_scatter | solution.py:293
  1612.3 160.1 %reduce-scatter.25.cloned.1.call-start = ((), (), s32[]{:S(2)}) async-start(), calls=%async_computation.36 | async-start | bytes 1114112 | tf_op jit(solution)/shard_map/reduce_scatter | solution.py:290
  1617.8 395.5 %reduce-scatter.43.cloned.1.call-start = ((), (), s32[]{:S(2)}) async-start(), calls=%async_computation.45 | async-start | bytes 2785280
  1779.0 236.2 %reduce-scatter.31.cloned.1.call-start = ((), (), s32[]{:S(2)}) async-start(), calls=%async_computation.39 | async-start | bytes 4456448 | tf_op jit(solution)/shard_map/reduce_scatter | solution.py:353
  1803.2 392.2 %reduce-scatter.39.cloned.1.call-start = ((), (), s32[]{:S(2)}) async-start(), calls=%async_computation.43 | async-start | bytes 12255232 | tf_op jit(solution)/shard_map/reduce_scatter | solution.py:368
  1811.2 631.8 %reduce-scatter.37.cloned.1.call-start = ((), (), s32[]{:S(2)}) async-start(), calls=%async_computation.42 | async-start | bytes 12255232 | tf_op jit(solution)/shard_map/reduce_scatter | solution.py:365
  1818.3 872.6 %reduce-scatter.35.cloned.1.call-start = ((), (), s32[]{:S(2)}) async-start(), calls=%async_computation.41 | async-start | bytes 12255232 | tf_op jit(solution)/shard_map/reduce_scatter | solution.py:362
  1825.4 1050.4 %reduce-scatter.33.cloned.1.call-start = ((), (), s32[]{:S(2)}) async-start(), calls=%async_computation.40 | async-start | bytes 8912896 | tf_op jit(solution)/shard_map/reduce_scatter | solution.py:356
  1832.3 1255.5 %reduce-scatter.29.cloned.1.call-start = ((), (), s32[]{:S(2)}) async-start(), calls=%async_computation.38 | async-start | bytes 13369344 | tf_op jit(solution)/shard_map/reduce_scatter | solution.py:344
  1847.8 1294.8 %reduce-scatter.47.cloned.1.call-start = ((), (), s32[]{:S(2)}) async-start(), calls=%async_computation.47 | async-start | bytes 8650752
  1904.0 1262.6 %reduce-scatter.45.cloned.1.call-start = ((), (), s32[]{:S(2)}) async-start(), calls=%async_computation.46 | async-start | bytes 8650752
  1957.3 1232.8 %reduce-scatter.41.cloned.1.call-start = ((), (), s32[]{:S(2)}) async-start(), calls=%async_computation.44 | async-start | bytes 8650752 | tf_op jit(solution)/shard_map/reduce_scatter | solution.py:391
  1971.3 1224.0 %all-reduce.9.cloned.1.call-start = ((), (), s32[]{:S(2)}) async-start(), calls=%async_computation.48 | async-start | bytes 7766016 | tf_op jit(solution)/shard_map/psum | solution.py:374
  2013.3 1074.6 %copy-start.152 = (f32[512]{0:T(512)S(1)}, f32[512]{0:T(512)}, u32[]{:S(2)}) copy-start(f32[512]{0:T(512)} %get-tuple-element.90) | copy-start | bytes 6148
  2013.3 1074.6 %copy-start.153 = (f32[512]{0:T(512)S(1)}, f32[512]{0:T(512)}, u32[]{:S(2)}) copy-start(f32[512]{0:T(512)} %get-tuple-element.88) | copy-start | bytes 6148
  2013.3 1075.2 %copy-start.7 = (bf16[2048,576]{0,1:T(8,128)(2,1)S(1)}, bf16[2048,576]{0,1:T(8,128)(2,1)}, u32[]{:S(2)}) copy-start(bf16[2048,576]{0,1:T(8,128)(2,1)} %all-gather.19.cloned.1.call-done) | copy-start | bytes 7077892
  2013.3 1075.2 %copy-start.108 = (bf16[64,512]{1,0:T(8,128)(2,1)S(1)}, bf16[64,512]{1,0:T(8,128)(2,1)}, u32[]{:S(2)}) copy-start(bf16[64,512]{1,0:T(8,128)(2,1)} %copy-done.107) | copy-start | bytes 196612
  (182 other events, 4523.0 us)
Sparse Core Ops, SparseCore 0:
  10.7 69.6 all-gather.18
  83.1 105.9 all-gather.16
  191.9 159.5 all-gather.14
  354.7 53.4 all-gather.20
  410.8 111.6 all-gather.22
  523.9 14.1 all-gather.34
  539.6 17.1 all-gather.32
  558.3 17.1 all-gather.30
  578.3 195.7 all-gather.26
  776.7 175.7 all-gather.24
  955.3 140.3 all-gather.28
  1161.8 90.8 reduce-scatter.20
  1268.7 60.0 all-gather.36
  1515.0 85.6 reduce-scatter.22
  1612.3 83.0 reduce-scatter.26
  1698.2 74.1 reduce-scatter.24
  1779.1 78.4 reduce-scatter.42
  1859.7 92.7 reduce-scatter.30
  1954.8 240.4 reduce-scatter.38
  2197.5 245.5 reduce-scatter.36
  2445.4 245.5 reduce-scatter.34
  2693.2 182.4 reduce-scatter.32
  2881.4 206.4 reduce-scatter.28
  3090.7 13.3 reduce-scatter.46
  3107.0 15.0 reduce-scatter.44
  3124.3 15.0 reduce-scatter.40
  3142.7 26.3 all-reduce.8
where the time goes:
time: 3220 us; the launch traced here: 3210 us
  waiting for transfers between devices  2000 us (62%)
  matrix products  393 us (12%)
  blocking collectives  345 us (11%)
  local copies, waits for them, and re-layouts  286 us (9%)
  starting transfers between devices  103 us (3%)
  other arithmetic  67.9 us (2%)
    reduce_scatter x1, waiting for transfers between devices, body(): lax.psum_scatter(dense_totals[7].astype(jnp.bfloat16), 'fsdp', scatter_di...  248 us
    reduce_scatter x1, waiting for transfers between devices, body(): lax.psum_scatter(dense_totals[8].astype(jnp.bfloat16), 'fsdp', scatter_di...  248 us
    dot_general x53, matrix products, contract(): return jnp.einsum(form, left, right, preferred_element_type=jnp.float32)  244 us
    reduce_scatter x1, waiting for transfers between devices, body(): lax.psum_scatter(dense_totals[1].astype(jnp.bfloat16), 'fsdp', scatter_di...  212 us
    reduce_scatter x1, waiting for transfers between devices, body(): lax.psum_scatter(dense_totals[5].astype(jnp.bfloat16), 'fsdp', scatter_di...  185 us
    reduce_scatter x1, waiting for transfers between devices, body(): lax.psum_scatter(dense_totals[9].astype(jnp.bfloat16), 'fsdp', scatter_di...  180 us
    all_gather x1, waiting for transfers between devices, body(): lax.all_gather(shared_gate, 'fsdp', axis=0, tiled=True)  170 us
    unnamed x409, local copies, waits for them, and re-layouts  158 us
  transfers between devices with their start and end apart: 35, of which 18 were waited for; matrix products, arithmetic and copies ran while one was open for 20% of the time, Pallas kernels for 0%

commit v1 on v0

v1 whole, which is shorter than its diff:
```python
import jax
import jax.numpy as jnp
from jax import lax
from jax.sharding import PartitionSpec as P

H = 16
DN = 128
DR = 64
DV = 128
R = 512
TOP = 6
MICRO = 2

EPS = 1e-06
THETA = 10000.0
NEG = -1e30
F32 = jnp.float32
BF16 = jnp.bfloat16


def contract(form, left, right):
    return jnp.einsum(form, left, right, preferred_element_type=F32)


def rms_forward(value, gain):
    factor = lax.rsqrt(jnp.mean(value * value, axis=-1, keepdims=True) + EPS)
    return (value * factor * gain, factor)


def rms_backward(value, factor, gain, grad):
    scaled = grad * gain
    inner = jnp.mean(value * scaled, axis=-1, keepdims=True)
    return (
        factor * scaled - value * factor * factor * factor * inner,
        jnp.sum(grad * value * factor, axis=0),
    )


def rope_tables(positions, width):
    half = width // 2
    freqs = THETA ** (-(2.0 * jnp.arange(half, dtype=F32)) / width)
    angles = positions.astype(F32)[:, None] * freqs[None, :]
    return (jnp.cos(angles), jnp.sin(angles))


def rotate(value, cosine, sine):
    half = value.shape[-1] // 2
    first = value[..., :half]
    second = value[..., half:]
    return jnp.concatenate(
        [first * cosine - second * sine, second * cosine + first * sine], axis=-1
    )


def rotate_back(grad, cosine, sine):
    half = grad.shape[-1] // 2
    first = grad[..., :half]
    second = grad[..., half:]
    return jnp.concatenate(
        [first * cosine + second * sine, second * cosine - first * sine], axis=-1
    )


def silu_slope(value):
    sigma = jax.nn.sigmoid(value)
    return sigma * (1.0 + value * (1.0 - sigma))


def partners(devices, k, i, j):
    outer = devices // 4
    return [
        (d, ((d // 4 + k) % outer) * 4 + ((d % 4) ^ (2 * i + j))) for d in range(devices)
    ]


def pull(value, devices, k, i, j):
    perm = [(there, here) for here, there in partners(devices, k, i, j)]
    return lax.ppermute(value, "fsdp", perm)


def push(value, devices, k, i, j):
    return lax.ppermute(value, "fsdp", partners(devices, k, i, j))


def outer_order(outer):
    near = []
    for k in range(1, outer):
        near.append((min(k, outer - k), k))
    return [k for _, k in sorted(near)]


def gather_blocks(block, devices):
    outer = devices // 4
    order = [0] + outer_order(outer)
    base = {0: block}
    for k in order[1:]:
        base[k] = pull(block, devices, k, 0, 0)
    held = {}
    for k in order:
        held[k, 0, 0] = base[k]
        held[k, 0, 1] = pull(base[k], devices, 0, 0, 1)
        held[k, 1, 0] = pull(base[k], devices, 0, 1, 0)
    for place, k in enumerate(order):
        if place % 2 == 0:
            held[k, 1, 1] = pull(held[k, 0, 1], devices, 0, 1, 0)
        else:
            held[k, 1, 1] = pull(held[k, 1, 0], devices, 0, 0, 1)
    return [held[k, i, j] for k in range(outer) for i in (0, 1) for j in (0, 1)]


def total(first, *others):
    value = first.astype(F32)
    for item in others:
        value = value + item.astype(F32)
    return value


def scatter_blocks(blocks, devices):
    outer = devices // 4
    order = outer_order(outer)[::-1] + [0]
    held = {}
    for k in range(outer):
        for i in (0, 1):
            for j in (0, 1):
                held[k, i, j] = blocks[4 * k + 2 * i + j]
    for place, k in enumerate(order):
        if place % 2 == 0:
            held[k, 0, 1] = total(held[k, 0, 1], push(held[k, 1, 1], devices, 0, 1, 0)).astype(BF16)
        else:
            held[k, 1, 0] = total(held[k, 1, 0], push(held[k, 1, 1], devices, 0, 0, 1)).astype(BF16)
    sums = {}
    for k in order:
        sums[k] = total(
            held[k, 0, 0],
            push(held[k, 0, 1], devices, 0, 0, 1),
            push(held[k, 1, 0], devices, 0, 1, 0),
        )
    return total(sums[0], *[push(sums[k].astype(BF16), devices, k, 0, 0) for k in order[:-1]])


def rep_pull(value, count, step):
    return lax.ppermute(value, "rep", [((d + step) % count, d) for d in range(count)])


def rep_parts(value, count):
    return [value] + [rep_pull(value, count, step) for step in range(1, count)]


def rep_total(parts, count):
    value = parts[0].astype(F32)
    for step in range(1, count):
        perm = [(d, (d + step) % count) for d in range(count)]
        value = value + lax.ppermute(parts[step], "rep", perm).astype(F32)
    return value


def body(
    hidden_in,
    cotangent,
    lengths,
    routes,
    gate_values,
    attn_gain,
    query_proj,
    latent_proj,
    latent_gain,
    expand_proj,
    output_proj,
    ffn_gain,
    shared_gate,
    shared_lift,
    shared_down,
    expert_gate,
    expert_lift,
    expert_down,
):
    tok = hidden_in.shape[1]
    width = hidden_in.shape[2]
    n = lax.axis_size("fsdp")
    reps = lax.axis_size("rep")
    me = lax.axis_index("fsdp")
    rep = lax.axis_index("rep")
    outer = n // 4
    seq = tok * n
    capacity = min(tok, 3 * tok * TOP // (2 * n))
    split = max(1, n // H)
    scale = (DN + DR) ** (-0.5)
    rows = width // n

    slots = jnp.arange(n, dtype=jnp.int32)
    abs_of_rel = ((me // 4 + slots // 4) % outer) * 4 + ((me % 4) ^ (slots % 4))
    rel_of_abs = ((slots // 4 - me // 4) % outer) * 4 + ((slots % 4) ^ (me % 4))
    rep_order = (jnp.arange(reps, dtype=jnp.int32) - rep) % reps
    own_pos = me * tok + jnp.arange(tok, dtype=jnp.int32)
    pos = (abs_of_rel[:, None] * tok + jnp.arange(tok, dtype=jnp.int32)[None, :]).reshape(seq)
    cosine, sine = rope_tables(pos, DR)

    def all_to_all(value):
        return lax.all_to_all(value, "fsdp", split_axis=0, concat_axis=0, tiled=True)

    def rep_slice(value, axis):
        size = value.shape[axis] // reps
        return lax.dynamic_slice_in_dim(value, rep * size, size, axis)

    def rep_join(value, axis):
        parts = jnp.take(jnp.stack(rep_parts(value, reps)), rep_order, axis=0)
        return jnp.concatenate([parts[i] for i in range(reps)], axis=axis)

    def reshard(value):
        return rep_join(all_to_all(rep_slice(value, 1)), 1)

    def unreshard(value):
        size = value.shape[1] // reps
        parts = [
            lax.dynamic_slice_in_dim(value, ((rep + step) % reps) * size, size, 1).astype(BF16)
            for step in range(reps)
        ]
        parts[0] = lax.dynamic_slice_in_dim(value, rep * size, size, 1)
        return rep_join(all_to_all(rep_total(parts, reps).astype(BF16)), 1).astype(F32)

    def by_head(value):
        return jnp.repeat(value, split, axis=0) if split > 1 else value

    hidden_all = [
        jnp.concatenate(gather_blocks(hidden_in[m], n), axis=0) for m in range(MICRO)
    ]

    gains = jnp.stack(
        [attn_gain, ffn_gain, jnp.pad(latent_gain, (0, rows - latent_gain.shape[0]))]
    )
    small = jnp.concatenate(
        [rep_slice(latent_proj.T, 0), jnp.pad(gains, ((0, 13), (0, 0)))], axis=0
    )
    small_all = jnp.take(jnp.stack(gather_blocks(small, n)), rel_of_abs, axis=0)
    part = small.shape[0] - 16
    latent_t = rep_join(
        jnp.transpose(small_all[:, :part], (1, 0, 2)).reshape(part, width), 0
    )
    attn_gain_f = small_all[:, part].reshape(width).astype(F32)
    ffn_gain_f = small_all[:, part + 1].reshape(width).astype(F32)
    latent_gain_f = small_all[:, part + 2, : latent_gain.shape[0]].reshape(R).astype(F32)

    query_w = reshard(
        by_head(jnp.transpose(query_proj.reshape(rows, H, DN + DR), (1, 0, 2)))
    ).reshape(width, DN + DR)
    expand_w = reshard(
        by_head(jnp.transpose(expand_proj.reshape(R // n, H, DN + DV), (1, 0, 2)))
    ).reshape(R, DN + DV)
    in_w = jnp.concatenate(
        [query_w[:, :DN], latent_t[:R].T, query_w[:, DN:], latent_t[R:].T], axis=1
    )

    att = []
    heads_local = []
    for m in range(MICRO):
        length = lengths[m]
        value = hidden_all[m].astype(F32)
        normed, factor = rms_forward(value, attn_gain_f)
        normed = normed.astype(BF16)
        mixed_in = contract("td,dj->tj", normed, in_w)
        latent = mixed_in[:, DN : DN + R]
        latent_norm, latent_factor = rms_forward(latent, latent_gain_f)
        latent_low = latent_norm.astype(BF16)
        q_rot = rotate(mixed_in[:, DN + R : DN + R + DR], cosine, sine)
        k_rot = rotate(mixed_in[:, DN + R + DR :], cosine, sine)
        kv = contract("tr,rj->tj", latent_low, expand_w)
        query = jnp.concatenate([mixed_in[:, :DN], q_rot], axis=1).astype(BF16)
        key = jnp.concatenate([kv[:, :DN], k_rot], axis=1).astype(BF16)
        val = kv[:, DN:].astype(BF16)
        visible = (pos[None, :] <= pos[:, None]) & (pos[None, :] < length)
        scores = jnp.where(visible, scale * contract("td,sd->ts", query, key), NEG)
        peak = jnp.max(scores, axis=-1, keepdims=True)
        raised = jnp.exp(scores - peak)
        probs = raised / jnp.sum(raised, axis=-1, keepdims=True)
        probs_low = probs.astype(BF16)
        out = contract("ts,sd->td", probs_low, val).astype(BF16)
        out = jnp.take(out.reshape(n, tok, DV), rel_of_abs, axis=0)
        out = all_to_all(out)[::split]
        heads_out = jnp.transpose(out, (1, 0, 2)).reshape(tok, n, H * DV // n)
        heads_local.append(jnp.take(heads_out, abs_of_rel, axis=1).reshape(tok, H * DV))
        att.append((value, factor, normed, latent[:tok], latent_factor[:tok], latent_low,
                    query, key, val, probs, probs_low))

    cols = width // reps
    out_blocks = gather_blocks(rep_slice(output_proj, 1), n)
    out_parts = rep_parts(jnp.concatenate(out_blocks, axis=0), reps)

    def columns(step):
        return ((rep + step) % reps) * cols

    grad_rows = []
    grad_all = []
    for m in range(MICRO):
        grad_rows.append(
            jnp.where((own_pos < lengths[m])[:, None], cotangent[m], jnp.zeros_like(cotangent[m]))
        )
        grad_all.append(jnp.concatenate(gather_blocks(grad_rows[m], n), axis=0))

    shared_in = jnp.concatenate(
        [
            jnp.transpose(shared_gate.reshape(rows, n, -1), (1, 0, 2)),
            jnp.transpose(shared_lift.reshape(rows, n, -1), (1, 0, 2)),
        ],
        axis=2,
    )
    units = shared_in.shape[2] // 2
    shared_in = reshard(shared_in).reshape(width, 2 * units)
    gate_parts = rep_parts(jnp.swapaxes(expert_gate[0], 0, 1), reps)
    lift_parts = rep_parts(jnp.swapaxes(expert_lift[0], 0, 1), reps)
    down_parts = rep_parts(expert_down[0], reps)

    dense_gate = jnp.sum(
        jnp.where(routes[..., None] == slots, gate_values[..., None], 0.0), axis=2
    )
    arrived_gate = all_to_all(jnp.transpose(dense_gate, (2, 0, 1)))
    arrived_gate = jnp.take(arrived_gate, abs_of_rel, axis=0)

    merge = 1
    while (merge * capacity) % 16:
        merge *= 2
    groups = n // merge
    span = merge * tok
    room = merge * capacity
    upper = (jnp.arange(span)[:, None] <= jnp.arange(span)[None, :]).astype(BF16)

    outputs = []
    input_grads = []
    part_ffn = 0.0
    keep = []
    for m in range(MICRO):
        hidden = hidden_in[m].astype(F32)
        residual = jnp.zeros((tok, width), F32)
        for step in range(reps):
            share = contract("tj,jd->td", heads_local[m], out_parts[step])
            residual = lax.dynamic_update_slice(residual, share, (0, columns(step)))
        residual = hidden + residual
        mixed, inv_second = rms_forward(residual, ffn_gain_f)
        mixed_all = jnp.concatenate(gather_blocks(mixed.astype(BF16), n), axis=0)

        gate_here = arrived_gate[:, m].reshape(groups, span)
        hit = gate_here > 0.0
        place = contract("gt,ts->gs", hit.astype(BF16), upper).astype(jnp.int32) - 1
        chosen = hit[:, None, :] & (
            place[:, None, :] == jnp.arange(room, dtype=jnp.int32)[None, :, None]
        )
        pick = chosen.astype(BF16)
        row_gate = jnp.sum(jnp.where(chosen, gate_here[:, None, :], 0.0), axis=2).reshape(-1, 1)

        def select(value):
            return contract("gct,gtd->gcd", pick, value.reshape(groups, span, width)).reshape(
                groups * room, width
            )

        def spread(value):
            return contract("gct,gcd->gtd", pick, value.reshape(groups, room, width)).reshape(
                seq, width
            )

        arrived = select(mixed_all).astype(BF16)
        back = (row_gate * select(grad_all[m])).astype(BF16)

        share_v = contract("td,df->tf", mixed_all, shared_in)
        share_g, share_u = share_v[:, :units], share_v[:, units:]
        shared_hidden = (jax.nn.silu(share_g) * share_u).astype(BF16)
        grad_shared = contract("td,fd->tf", grad_all[m], shared_down)
        grad_sgu = jnp.concatenate(
            [
                (grad_shared * share_u * silu_slope(share_g)).astype(BF16),
                (grad_shared * jax.nn.silu(share_g)).astype(BF16),
            ],
            axis=1,
        )

        expert_out = 0.0
        grad_arrived = 0.0
        eh, eg, eu = [], [], []
        for step in range(reps):
            gate_v = contract("cd,fd->cf", arrived, gate_parts[step])
            lift_v = contract("cd,fd->cf", arrived, lift_parts[step])
            grad_eh = contract("cd,fd->cf", back, down_parts[step])
            eh.append((jax.nn.silu(gate_v) * lift_v).astype(BF16))
            eg.append((grad_eh * lift_v * silu_slope(gate_v)).astype(BF16))
            eu.append((grad_eh * jax.nn.silu(gate_v)).astype(BF16))
            grad_arrived = grad_arrived + (
                contract("cf,fd->cd", eg[step], gate_parts[step])
                + contract("cf,fd->cd", eu[step], lift_parts[step])
            )
        grad_mixed_part = (
            spread(grad_arrived.astype(BF16)) + contract("tf,df->td", grad_sgu, shared_in)
        ).astype(BF16)
        grad_mixed = scatter_blocks(
            [grad_mixed_part[s * tok : (s + 1) * tok] for s in range(n)], n
        )
        for step in range(reps):
            expert_out = expert_out + contract("cf,fd->cd", eh[step], down_parts[step])
        out_part = (
            spread((row_gate * expert_out.astype(BF16).astype(F32)).astype(BF16))
            + contract("tf,fd->td", shared_hidden, shared_down)
        ).astype(BF16)
        routed = scatter_blocks([out_part[s * tok : (s + 1) * tok] for s in range(n)], n)
        outputs.append((residual + routed).astype(BF16))

        grad_res, ffn = rms_backward(residual, inv_second, ffn_gain_f, grad_mixed)
        part_ffn = part_ffn + ffn
        grad_res = grad_res + grad_rows[m].astype(F32)
        grad_res_low = grad_res.astype(BF16)
        grad_heads = 0.0
        for step in range(reps):
            piece = lax.dynamic_slice_in_dim(grad_res_low, columns(step), cols, 1)
            grad_heads = grad_heads + contract("td,jd->tj", piece, out_parts[step])
        keep.append((arrived, back, eh, eg, eu, mixed_all, shared_hidden, grad_sgu,
                     grad_res, grad_res_low, grad_heads.astype(BF16)))

    def joined(index):
        return jnp.concatenate([item[index] for item in keep], axis=0)

    def joined_step(index, step):
        return jnp.concatenate([item[index][step] for item in keep], axis=0)

    all_ar, all_ba = joined(0), joined(1)

    def expert_total(form, index, other):
        parts = [contract(form, joined_step(index, step), other) for step in range(reps)]
        return rep_total([parts[0]] + [item.astype(BF16) for item in parts[1:]], reps)

    grad_expert_gate = jnp.swapaxes(expert_total("cf,cd->fd", 3, all_ar), 0, 1)[None]
    grad_expert_lift = jnp.swapaxes(expert_total("cf,cd->fd", 4, all_ar), 0, 1)[None]
    grad_expert_down = expert_total("cf,cd->fd", 2, all_ba)[None]

    all_mx = joined(5)
    grad_shared_in = unreshard(
        contract("td,tf->df", all_mx, joined(7)).reshape(n, rows, 2 * units)
    )
    grad_shared_gate = jnp.transpose(grad_shared_in[:, :, :units], (1, 0, 2)).reshape(rows, -1)
    grad_shared_lift = jnp.transpose(grad_shared_in[:, :, units:], (1, 0, 2)).reshape(rows, -1)
    down_sum = contract("tf,td->fd", joined(6), jnp.concatenate(grad_all, axis=0))
    grad_shared_down = down_sum + sum(
        rep_pull(down_sum.astype(BF16), reps, step).astype(F32) for step in range(1, reps)
    )

    grad_in_w = 0.0
    grad_expand_w = 0.0
    part_attn = 0.0
    part_latent = 0.0
    grad_kvs = []
    normed_first = []
    for m in range(MICRO):
        (value, factor, normed, latent, latent_factor, latent_low,
         query, key, val, probs, probs_low) = att[m]
        grad_heads = jnp.take(keep[m][10].reshape(tok, n, H * DV // n), rel_of_abs, axis=1)
        grad_heads = by_head(jnp.transpose(grad_heads.reshape(tok, H, DV), (1, 0, 2)))
        grad_heads = jnp.take(all_to_all(grad_heads), abs_of_rel, axis=0).reshape(seq, DV)
        if split > 1:
            grad_heads = jnp.where(me % split == 0, grad_heads, jnp.zeros_like(grad_heads))
        grad_probs = contract("td,sd->ts", grad_heads, val)
        grad_scores = (
            probs * (grad_probs - jnp.sum(probs * grad_probs, axis=-1, keepdims=True))
        ).astype(BF16)
        grad_query = scale * contract("ts,sd->td", grad_scores, key)
        grad_key = scale * contract("ts,td->sd", grad_scores, query)
        grad_val = contract("ts,td->sd", probs_low, grad_heads)
        grad_query = jnp.concatenate(
            [grad_query[:, :DN], rotate_back(grad_query[:, DN:], cosine, sine)], axis=1
        ).astype(BF16)
        grad_kv = jnp.concatenate([grad_key[:, :DN], grad_val], axis=1).astype(BF16)
        grad_latent_part = jnp.concatenate(
            [contract("tj,rj->tr", grad_kv, expand_w), grad_key[:, DN:]], axis=1
        ).astype(BF16)
        grad_latent = scatter_blocks(
            [grad_latent_part[s * tok : (s + 1) * tok] for s in range(n)], n
        )
        grad_normed_part = contract("tj,dj->td", grad_query, query_w)
        part_attn = part_attn + jnp.sum(grad_normed_part * value * factor, axis=0)
        grad_normed_part = grad_normed_part.astype(BF16)
        grad_normed = scatter_blocks(
            [grad_normed_part[s * tok : (s + 1) * tok] for s in range(n)], n
        )
        grad_in_w = grad_in_w + contract("td,tj->dj", normed, grad_query)
        grad_expand_w = grad_expand_w + contract("tr,tj->rj", latent_low, grad_kv)

        grad_c, latent_sum = rms_backward(
            latent, latent_factor, latent_gain_f, grad_latent[:, :R]
        )
        part_latent = part_latent + latent_sum
        grad_krope = rotate_back(grad_latent[:, R:], cosine[:tok], sine[:tok])
        grad_kva = jnp.concatenate([grad_c, grad_krope], axis=1).astype(BF16)
        grad_kvs.append(grad_kva)
        grad_local = contract("tj,jd->td", grad_kva, latent_t)
        part_attn = part_attn + jnp.sum(grad_local * value[:tok] * factor[:tok], axis=0)
        grad_first, _ = rms_backward(
            value[:tok], factor[:tok], attn_gain_f, grad_normed + grad_local
        )
        input_grads.append((grad_first + keep[m][8]).astype(BF16))

    grad_query_proj = jnp.transpose(
        unreshard(grad_in_w.reshape(n, rows, DN + DR))[::split], (1, 0, 2)
    ).reshape(rows, H * (DN + DR))
    grad_expand_proj = jnp.transpose(
        unreshard(grad_expand_w.reshape(n, R // n, DN + DV))[::split], (1, 0, 2)
    ).reshape(R // n, H * (DN + DV))

    kv_blocks = gather_blocks(jnp.concatenate(grad_kvs, axis=0), n)
    latent_total = 0.0
    for m in range(MICRO):
        kv_all = jnp.concatenate([item[m * tok : (m + 1) * tok] for item in kv_blocks], axis=0)
        piece = lax.dynamic_slice_in_dim(att[m][2], me * rows, rows, 1)
        latent_total = latent_total + contract("tj,td->jd", kv_all, piece)
    latent_total = latent_total + sum(
        rep_pull(latent_total.astype(BF16), reps, step).astype(F32) for step in range(1, reps)
    )
    grad_latent_proj = latent_total.T

    all_ho = jnp.concatenate(heads_local, axis=0)
    all_gr = joined(9)
    shares = []
    for step in range(reps):
        piece = lax.dynamic_slice_in_dim(all_gr, columns(step), cols, 1)
        shares.append(contract("tj,td->jd", all_ho, piece))
    out_total = rep_total([shares[0]] + [item.astype(BF16) for item in shares[1:]], reps)
    out_total = out_total.astype(BF16).reshape(n, rows, cols)
    out_total = scatter_blocks([out_total[s] for s in range(n)], n).astype(BF16)
    grad_output_proj = rep_join(out_total, 1).astype(F32)

    gain_parts = jnp.stack(
        [
            part_attn.reshape(n, rows),
            part_ffn.reshape(n, rows),
            jnp.pad(part_latent.reshape(n, R // n), ((0, 0), (0, rows - R // n))),
        ],
        axis=1,
    )
    gain_sum = jnp.sum(all_to_all(gain_parts), axis=0)
    gain_sum = gain_sum + sum(rep_pull(gain_sum, reps, step) for step in range(1, reps))

    return (
        jnp.stack(outputs),
        jnp.stack(input_grads),
        gain_sum[0],
        grad_query_proj,
        grad_latent_proj,
        gain_sum[2, : R // n],
        grad_expand_proj,
        grad_output_proj,
        gain_sum[1],
        grad_shared_gate,
        grad_shared_lift,
        grad_shared_down,
        grad_expert_gate,
        grad_expert_lift,
        grad_expert_down,
    )


def solution(mesh):
    in_specs = (
        P("rep", "fsdp", None),
        P("rep", "fsdp", None),
        P("rep"),
        P("rep", "fsdp", None),
        P("rep", "fsdp", None),
        P("fsdp"),
        P("fsdp", None),
        P("fsdp", None),
        P("fsdp"),
        P("fsdp", None),
        P("fsdp", None),
        P("fsdp"),
        P("fsdp", None),
        P("fsdp", None),
        P("fsdp", None),
        P("fsdp", None, "rep"),
        P("fsdp", None, "rep"),
        P("fsdp", "rep", None),
    )
    out_specs = (
        P("rep", "fsdp", None),
        P("rep", "fsdp", None),
        P("fsdp"),
        P("fsdp", None),
        P("fsdp", None),
        P("fsdp"),
        P("fsdp", None),
        P("fsdp", None),
        P("fsdp"),
        P("fsdp", None),
        P("fsdp", None),
        P("fsdp", None),
        P("fsdp", None, "rep"),
        P("fsdp", None, "rep"),
        P("fsdp", "rep", None),
    )
    return jax.shard_map(body, mesh=mesh, in_specs=in_specs, out_specs=out_specs, check_vma=False)
```

time: 3220 us -> 1390 us (0.43)
  waiting for transfers between devices: 2000 us -> 372 us
  blocking collectives: 345 us -> 0 us
  starting transfers between devices: 103 us -> 403 us
  matrix products: 393 us -> 259 us
  local copies, waits for them, and re-layouts: 286 us -> 209 us
  other arithmetic: 67.9 us -> 126 us
    reduce_scatter x11 -> x0, waiting for transfers between devices: 1230 us -> none  [the longest x1 248 us: body(): lax.psum_scatter(dense_totals[7].astype(jnp.bfloat16), 'fsdp', scatter_di...]
    all_gather x12 -> x0, waiting for transfers between devices: 557 us -> none  [the longest x1 170 us: body(): lax.all_gather(shared_gate, 'fsdp', axis=0, tiled=True)]
    ppermute x0 -> x292, starting transfers between devices: none -> 340 us  [the longest x135 169 us: pull(): return lax.ppermute(value, 'fsdp', perm)]
    ppermute x0 -> x292, waiting for transfers between devices: none -> 339 us  [the longest x135 199 us: pull(): return lax.ppermute(value, 'fsdp', perm)]
    all_gather x4 -> x0, blocking collectives: 257 us -> none  [the longest x2 131 us: body(): lax.all_gather(key_rot, 'fsdp', axis=0, tiled=True)]
    all_to_all x8 -> x12, waiting for transfers between devices: 210 us -> 33.2 us  [all_to_all(): lax.all_to_all(value, 'fsdp', split_axis=0, concat_axis=0, tiled=True)]
    dot_general x77 -> x87, matrix products: 380 us -> 252 us  [contract(): return jnp.einsum(form, left, right, preferred_element_type=F32)]
    unnamed x2 -> x0, blocking collectives: 85.4 us -> none
  transfers between devices with their start and end apart: 35 -> 304, of which waited for: 18 -> 118; matrix products, arithmetic and copies ran while one was open for 20% -> 40% of each run, Pallas kernels for 0% -> 0%
where the time goes in v1:
time: 1390 us; the launch traced here: 1370 us
  starting transfers between devices  403 us (29%)
  waiting for transfers between devices  372 us (27%)
  matrix products  259 us (19%)
  local copies, waits for them, and re-layouts  209 us (15%)
  other arithmetic  126 us (9%)
    dot_general x87, matrix products, contract(): return jnp.einsum(form, left, right, preferred_element_type=F32)  252 us
    ppermute x135, waiting for transfers between devices, pull(): return lax.ppermute(value, 'fsdp', perm)  199 us
    ppermute x135, starting transfers between devices, pull(): return lax.ppermute(value, 'fsdp', perm)  169 us
    ppermute x135, starting transfers between devices, push(): return lax.ppermute(value, 'fsdp', partners(devices, k, i, j))  168 us
    ppermute x135, waiting for transfers between devices, push(): return lax.ppermute(value, 'fsdp', partners(devices, k, i, j))  140 us
    unnamed x577, local copies, waits for them, and re-layouts  125 us
    all_to_all x12, starting transfers between devices, all_to_all(): lax.all_to_all(value, 'fsdp', split_axis=0, concat_axis=0, tiled=True)  62.8 us
    all_to_all x12, waiting for transfers between devices, all_to_all(): lax.all_to_all(value, 'fsdp', split_axis=0, concat_axis=0, tiled=True)  33.2 us
  transfers between devices with their start and end apart: 304, of which 118 were waited for; matrix products, arithmetic and copies ran while one was open for 40% of the time, Pallas kernels for 0%

profile of v1, /device:TPU:0, one launch (start us, length us, event | category | flops | bytes accessed | tf_op | source)
XLA Modules:
  0.0 1374.2 jit_solution(15861335385381560613)
XLA Ops:
  45.6 6.9 all-to-all-start.1
  122.9 5.8 all-to-all-start
  136.5 5.7 collective-permute-done.131
  162.8 5.6 collective-permute-done.87
  180.5 5.0 collective-permute-done.35
  211.3 7.8 collective-permute-done.93
  229.5 5.2 collective-permute-done.10
  274.5 5.5 collective-permute-done.138
  328.5 6.8 convert_element_type.1162
  344.7 5.3 collective-permute-done.191
  363.3 7.5 collective-permute-start.199
  439.7 6.0 multiply_convert_fusion.2
  457.3 5.3 all-to-all-done.2
  476.9 5.3 fusion.349
  506.9 6.4 collective-permute-done.56
  516.0 7.2 collective-permute-done.60
  570.6 5.4 multiply_convert_fusion.15
  639.9 5.1 collective-permute-done.73
  660.5 7.3 collective-permute-done.100
  677.7 6.8 collective-permute-done.104
  721.1 5.3 convolution_convert_fusion.1
  726.5 5.4 convolution_convert_fusion.2
  731.9 5.8 convolution_convert_fusion.3
  737.7 4.8 multiply_convert_fusion.23
  752.5 6.0 fusion.350
  758.6 5.7 add_convert_fusion.1
  765.7 7.2 fusion.61
  876.3 6.6 all-to-all-start.7
  885.7 5.8 all-to-all-done.7
  891.5 5.8 all-to-all-start.6
  998.3 5.2 collective-permute-start.183
  1069.1 7.5 all-to-all-start.11
  1151.8 4.9 collective-permute-start.224
  1173.8 7.1 collective-permute-done.228
  1182.1 15.9 %collective-permute-done.164 = bf16[64,2048]{1,0:T(8,128)(2,1)S(1)} collective-permute-done((bf16[64,2048]{1,0:T(8,128)(2,1)}, bf16[64,2048]{1,0:T(8,128)(2,1)S(1)}, u32[]{:S(2)}, u32[]{:S(2)}) %collective-permute-start.164) | collective-permute-done | bytes 262176 | tf_op jit(solution)/shard_map/ppermute | solution.py:82
  1198.0 5.5 collective-permute-start.78
  1203.6 8.5 collective-permute-start.82
  1220.2 9.1 collective-permute-start.123
  1234.9 6.9 collective-permute-done.127
  1243.5 6.5 all-to-all-start.8
  1250.8 6.6 all-to-all-done.8
  1264.1 10.7 all-to-all-done.9
  1304.3 5.9 collective-permute-done.271
  1321.1 4.8 collective-permute-done.275
  1332.1 9.9 add_bitcast_fusion
  1350.1 7.3 add_bitcast_fusion.1
  1357.3 7.5 collective-permute-done.276
  1366.1 5.8 add_bitcast_fusion.2
  (1479 shorter events, 1053.2 us)
Async XLA Ops:
  3.1 52.6 %collective-permute-start.15 = (bf16[304,128]{1,0:T(8,128)(2,1)S(1)}, bf16[304,128]{1,0:T(8,128)(2,1)}, u32[]{:S(2)}, u32[]{:S(2)}) collective-permute-start(bf16[304,128]{1,0:T(8,128)(2,1)S(1)} %pad_maximum_fusion.53), channel_id=1, source_target_pairs={{1,0},{0,1},{3,2},{2,3},{5,4},{4,5},{7,6},{6,7},{9,8},{8,9},{11,10... | collective-permute-start | bytes 233480 | tf_op jit(solution)/shard_map/ppermute | solution.py:78
  6.1 53.1 %collective-permute-start.16 = (bf16[304,128]{1,0:T(8,128)(2,1)S(1)}, bf16[304,128]{1,0:T(8,128)(2,1)}, u32[]{:S(2)}, u32[]{:S(2)}) collective-permute-start(bf16[304,128]{1,0:T(8,128)(2,1)S(1)} %pad_maximum_fusion.53), channel_id=1, source_target_pairs={{2,0},{3,1},{0,2},{1,3},{6,4},{7,5},{4,6},{5,7},{10,8},{11,9},{8,1... | collective-permute-start | bytes 233480 | tf_op jit(solution)/shard_map/ppermute | solution.py:78
  7.6 53.0 %collective-permute-start.18 = (bf16[304,128]{1,0:T(8,128)(2,1)S(1)}, bf16[304,128]{1,0:T(8,128)(2,1)}, u32[]{:S(2)}, u32[]{:S(2)}) collective-permute-start(bf16[304,128]{1,0:T(8,128)(2,1)S(1)} %pad_maximum_fusion.53), channel_id=1, source_target_pairs={{4,0},{5,1},{6,2},{7,3},{8,4},{9,5},{10,6},{11,7},{12,8},{13,9},{1... | collective-permute-start | bytes 233480 | tf_op jit(solution)/shard_map/ppermute | solution.py:78
  11.2 56.8 %collective-permute-start.22 = (bf16[304,128]{1,0:T(8,128)(2,1)S(1)}, bf16[304,128]{1,0:T(8,128)(2,1)}, u32[]{:S(2)}, u32[]{:S(2)}) collective-permute-start(bf16[304,128]{1,0:T(8,128)(2,1)S(1)} %pad_maximum_fusion.53), channel_id=1, source_target_pairs={{8,0},{9,1},{10,2},{11,3},{12,4},{13,5},{14,6},{15,7},{0,8},{1,9},... | collective-permute-start | bytes 233480 | tf_op jit(solution)/shard_map/ppermute | solution.py:78
  11.2 72.1 %collective-permute-start.26 = (bf16[304,128]{1,0:T(8,128)(2,1)S(1)}, bf16[304,128]{1,0:T(8,128)(2,1)S(1)}, u32[]{:S(2)}, u32[]{:S(2)}) collective-permute-start(bf16[304,128]{1,0:T(8,128)(2,1)S(1)} %pad_maximum_fusion.53), channel_id=1, source_target_pairs={{12,0},{13,1},{14,2},{15,3},{0,4},{1,5},{2,6},{3,7},{4,8},{5,9},{6... | collective-permute-start | bytes 233480 | tf_op jit(solution)/shard_map/ppermute | solution.py:78
  45.6 77.3 %all-to-all-start.1 = ((bf16[16,16,256]{2,1,0:T(8,128)(2,1)}), bf16[16,16,256]{2,1,0:T(8,128)(2,1)S(1)}, u32[]{:S(2)}, u32[]{:S(2)}) async-start(bf16[16,16,256]{2,1,0:T(8,128)(2,1)} %bitcast.394), calls=%async_computation.1 | async-start | bytes 262144 | tf_op jit(solution)/shard_map/all_to_all | solution.py:199
  55.6 55.9 %collective-permute-start.83 = (bf16[64,2048]{1,0:T(8,128)(2,1)}, bf16[64,2048]{1,0:T(8,128)(2,1)S(1)}, u32[]{:S(2)}, u32[]{:S(2)}) collective-permute-start(bf16[64,2048]{1,0:T(8,128)(2,1)} %get-tuple-element.348), channel_id=1, source_target_pairs={{1,0},{0,1},{3,2},{2,3},{5,4},{4,5},{7,6},{6,7},{9,8},{8,9},{11,10... | collective-permute-start | bytes 786440 | tf_op jit(solution)/shard_map/ppermute | solution.py:78
  68.0 45.3 %collective-permute-start.84 = (bf16[64,2048]{1,0:T(8,128)(2,1)}, bf16[64,2048]{1,0:T(8,128)(2,1)}, u32[]{:S(2)}, u32[]{:S(2)}) collective-permute-start(bf16[64,2048]{1,0:T(8,128)(2,1)} %get-tuple-element.348), channel_id=1, source_target_pairs={{2,0},{3,1},{0,2},{1,3},{6,4},{7,5},{4,6},{5,7},{10,8},{11,9},{8,1... | collective-permute-start | bytes 786440 | tf_op jit(solution)/shard_map/ppermute | solution.py:78
  77.7 77.9 %collective-permute-start.86 = (bf16[64,2048]{1,0:T(8,128)(2,1)}, bf16[64,2048]{1,0:T(8,128)(2,1)}, u32[]{:S(2)}, u32[]{:S(2)}) collective-permute-start(bf16[64,2048]{1,0:T(8,128)(2,1)} %get-tuple-element.348), channel_id=1, source_target_pairs={{4,0},{5,1},{6,2},{7,3},{8,4},{9,5},{10,6},{11,7},{12,8},{13,9},{1... | collective-permute-start | bytes 786440 | tf_op jit(solution)/shard_map/ppermute | solution.py:78
  107.4 84.0 %collective-permute-start.90 = (bf16[64,2048]{1,0:T(8,128)(2,1)}, bf16[64,2048]{1,0:T(8,128)(2,1)}, u32[]{:S(2)}, u32[]{:S(2)}) collective-permute-start(bf16[64,2048]{1,0:T(8,128)(2,1)} %get-tuple-element.348), channel_id=1, source_target_pairs={{8,0},{9,1},{10,2},{11,3},{12,4},{13,5},{14,6},{15,7},{0,8},{1,9},... | collective-permute-start | bytes 786440 | tf_op jit(solution)/shard_map/ppermute | solution.py:78
  109.2 113.3 %collective-permute-start.94 = (bf16[64,2048]{1,0:T(8,128)(2,1)}, bf16[64,2048]{1,0:T(8,128)(2,1)}, u32[]{:S(2)}, u32[]{:S(2)}) collective-permute-start(bf16[64,2048]{1,0:T(8,128)(2,1)} %get-tuple-element.348), channel_id=1, source_target_pairs={{12,0},{13,1},{14,2},{15,3},{0,4},{1,5},{2,6},{3,7},{4,8},{5,9},{6... | collective-permute-start | bytes 786440 | tf_op jit(solution)/shard_map/ppermute | solution.py:78
  122.9 197.0 %all-to-all-start = ((bf16[16,64,192]{2,1,0:T(8,128)(2,1)}), bf16[16,64,192]{2,1,0:T(8,128)(2,1)S(1)}, u32[]{:S(2)}, u32[]{:S(2)}) async-start(bf16[16,64,192]{2,1,0:T(8,128)(2,1)} %copy.161), calls=%async_computation | async-start | bytes 1048576 | tf_op jit(solution)/shard_map/all_to_all | solution.py:199
  191.4 36.0 %collective-permute-start.11 = (bf16[64,2048]{1,0:T(8,128)(2,1)S(1)}, bf16[64,2048]{1,0:T(8,128)(2,1)S(1)}, u32[]{:S(2)}, u32[]{:S(2)}) collective-permute-start(bf16[64,2048]{1,0:T(8,128)(2,1)S(1)} %copy-done.140), channel_id=1, source_target_pairs={{12,0},{13,1},{14,2},{15,3},{0,4},{1,5},{2,6},{3,7},{4,8},{5,9},{6... | collective-permute-start | bytes 786440 | tf_op jit(solution)/shard_map/ppermute | solution.py:78
  205.6 66.0 %collective-permute-start.40 = (bf16[128,1024]{1,0:T(8,128)(2,1)S(1)}, bf16[128,1024]{1,0:T(8,128)(2,1)S(1)}, u32[]{:S(2)}, u32[]{:S(2)}) collective-permute-start(bf16[128,1024]{1,0:T(8,128)(2,1)S(1)} %copy-done.139), channel_id=1, source_target_pairs={{8,0},{9,1},{10,2},{11,3},{12,4},{13,5},{14,6},{15,7},{0,8},{1,9},... | collective-permute-start | bytes 786440 | tf_op jit(solution)/shard_map/ppermute | solution.py:78
  247.5 36.9 %collective-permute-start.44 = (bf16[128,1024]{1,0:T(8,128)(2,1)S(1)}, bf16[128,1024]{1,0:T(8,128)(2,1)}, u32[]{:S(2)}, u32[]{:S(2)}) collective-permute-start(bf16[128,1024]{1,0:T(8,128)(2,1)S(1)} %copy-done.139), channel_id=1, source_target_pairs={{12,0},{13,1},{14,2},{15,3},{0,4},{1,5},{2,6},{3,7},{4,8},{5,9},{6... | collective-permute-start | bytes 786440 | tf_op jit(solution)/shard_map/ppermute | solution.py:78
  265.2 301.3 %collective-permute-start.65 = (bf16[704,2048]{1,0:T(8,128)(2,1)}, bf16[704,2048]{1,0:T(8,128)(2,1)}, u32[]{:S(2)}, u32[]{:S(2)}) collective-permute-start(bf16[704,2048]{1,0:T(8,128)(2,1)} %bitcast.57), channel_id=1, source_target_pairs={{16,0},{0,16},{17,1},{1,17},{18,2},{2,18},{19,3},{3,19},{20,4},{4,... | collective-permute-start | bytes 8650760 | tf_op jit(solution)/shard_map/ppermute | solution.py:142
  302.9 70.7 %collective-permute-start.31 = (bf16[288,2048]{1,0:T(8,128)(2,1)}, bf16[288,2048]{1,0:T(8,128)(2,1)}, u32[]{:S(2)}, u32[]{:S(2)}) collective-permute-start(bf16[288,2048]{1,0:T(8,128)(2,1)} %bitcast.391), channel_id=1, source_target_pairs={{16,0},{0,16},{17,1},{1,17},{18,2},{2,18},{19,3},{3,19},{20,4},{4,... | collective-permute-start | bytes 3538952 | tf_op jit(solution)/shard_map/ppermute | solution.py:142
  319.9 114.8 %all-to-all-start.4 = ((bf16[16,64,352]{2,1,0:T(8,128)(2,1)}), bf16[16,64,352]{2,1,0:T(8,128)(2,1)}, u32[]{:S(2)}, u32[]{:S(2)}) async-start(bf16[16,64,352]{2,1,0:T(8,128)(2,1)} %copy.172), calls=%async_computation.4 | async-start | bytes 1572864 | tf_op jit(solution)/shard_map/all_to_all | solution.py:199
  361.5 115.4 %collective-permute-start.66 = (bf16[704,2048]{1,0:T(8,128)(2,1)}, bf16[704,2048]{1,0:T(8,128)(2,1)}, u32[]{:S(2)}, u32[]{:S(2)}) collective-permute-start(bf16[704,2048]{1,0:T(8,128)(2,1)} %bitcast.485), channel_id=1, source_target_pairs={{16,0},{0,16},{17,1},{1,17},{18,2},{2,18},{19,3},{3,19},{20,4},{4,... | collective-permute-start | bytes 8650760 | tf_op jit(solution)/shard_map/ppermute | solution.py:142
  363.3 51.5 %collective-permute-start.199 = (bf16[64,2048]{1,0:T(8,128)(2,1)}, bf16[64,2048]{1,0:T(8,128)(2,1)}, u32[]{:S(2)}, u32[]{:S(2)}) collective-permute-start(bf16[64,2048]{1,0:T(8,128)(2,1)} %get-tuple-element.129), channel_id=1, source_target_pairs={{12,0},{13,1},{14,2},{15,3},{0,4},{1,5},{2,6},{3,7},{4,8},{5,9},{6... | collective-permute-start | bytes 786440 | tf_op jit(solution)/shard_map/ppermute | solution.py:78
  370.8 44.0 %collective-permute-start.196 = (bf16[64,2048]{1,0:T(8,128)(2,1)}, bf16[64,2048]{1,0:T(8,128)(2,1)}, u32[]{:S(2)}, u32[]{:S(2)}) collective-permute-start(bf16[64,2048]{1,0:T(8,128)(2,1)} %collective-permute-done.195), channel_id=1, source_target_pairs={{1,0},{0,1},{3,2},{2,3},{5,4},{4,5},{7,6},{6,7},{9,8},{8,9},{11,10... | collective-permute-start | bytes 786440 | tf_op jit(solution)/shard_map/ppermute | solution.py:78
  373.7 36.3 %collective-permute-start.194 = (bf16[64,2048]{1,0:T(8,128)(2,1)}, bf16[64,2048]{1,0:T(8,128)(2,1)}, u32[]{:S(2)}, u32[]{:S(2)}) collective-permute-start(bf16[64,2048]{1,0:T(8,128)(2,1)} %collective-permute-done.193), channel_id=1, source_target_pairs={{1,0},{0,1},{3,2},{2,3},{5,4},{4,5},{7,6},{6,7},{9,8},{8,9},{11,10... | collective-permute-start | bytes 786440 | tf_op jit(solution)/shard_map/ppermute | solution.py:78
  414.8 155.8 %collective-permute-start.64 = (bf16[704,2048]{1,0:T(8,128)(2,1)}, bf16[704,2048]{1,0:T(8,128)(2,1)}, u32[]{:S(2)}, u32[]{:S(2)}) collective-permute-start(bf16[704,2048]{1,0:T(8,128)(2,1)} %bitcast.484), channel_id=1, source_target_pairs={{16,0},{0,16},{17,1},{1,17},{18,2},{2,18},{19,3},{3,19},{20,4},{4,... | collective-permute-start | bytes 8650760 | tf_op jit(solution)/shard_map/ppermute | solution.py:142
  433.8 52.4 %collective-permute-start.48 = (bf16[2048,1024]{1,0:T(8,128)(2,1)}, bf16[2048,1024]{1,0:T(8,128)(2,1)}, u32[]{:S(2)}, u32[]{:S(2)}) collective-permute-start(bf16[2048,1024]{1,0:T(8,128)(2,1)} %constant_dynamic-update-slice_fusion.32), channel_id=1, source_target_pairs={{16,0},{0,16},{17,1},{1,17},{18,2},{2,18},{19,3},{3,19},{20,4},{4,... | collective-permute-start | bytes 12582920 | tf_op jit(solution)/shard_map/ppermute | solution.py:142
  543.3 80.8 %collective-permute-start.98 = (bf16[64,2048]{1,0:T(8,128)(2,1)S(1)}, bf16[64,2048]{1,0:T(8,128)(2,1)S(1)}, u32[]{:S(2)}, u32[]{:S(2)}) collective-permute-start(bf16[64,2048]{1,0:T(8,128)(2,1)S(1)} %get-tuple-element.133), channel_id=1, source_target_pairs={{1,0},{0,1},{3,2},{2,3},{5,4},{4,5},{7,6},{6,7},{9,8},{8,9},{11,10... | collective-permute-start | bytes 786440 | tf_op jit(solution)/shard_map/ppermute | solution.py:78
  655.6 135.0 %collective-permute-start.143 = (bf16[64,2048]{1,0:T(8,128)(2,1)}, bf16[64,2048]{1,0:T(8,128)(2,1)}, u32[]{:S(2)}, u32[]{:S(2)}) collective-permute-start(bf16[64,2048]{1,0:T(8,128)(2,1)} %get-tuple-element.184), channel_id=1, source_target_pairs={{0,1},{1,0},{2,3},{3,2},{4,5},{5,4},{6,7},{7,6},{8,9},{9,8},{10,11... | collective-permute-start | bytes 786440 | tf_op jit(solution)/shard_map/ppermute | solution.py:82
  669.6 122.1 %collective-permute-start.145 = (bf16[64,2048]{1,0:T(8,128)(2,1)}, bf16[64,2048]{1,0:T(8,128)(2,1)}, u32[]{:S(2)}, u32[]{:S(2)}) collective-permute-start(bf16[64,2048]{1,0:T(8,128)(2,1)} %get-tuple-element.192), channel_id=1, source_target_pairs={{0,2},{1,3},{2,0},{3,1},{4,6},{5,7},{6,4},{7,5},{8,10},{9,11},{10,... | collective-permute-start | bytes 786440 | tf_op jit(solution)/shard_map/ppermute | solution.py:82
  691.3 101.3 %collective-permute-start.149 = (bf16[64,2048]{1,0:T(8,128)(2,1)}, bf16[64,2048]{1,0:T(8,128)(2,1)}, u32[]{:S(2)}, u32[]{:S(2)}) collective-permute-start(bf16[64,2048]{1,0:T(8,128)(2,1)} %get-tuple-element.196), channel_id=1, source_target_pairs={{0,8},{1,9},{2,10},{3,11},{4,12},{5,13},{6,14},{7,15},{8,0},{9,1},... | collective-permute-start | bytes 786440 | tf_op jit(solution)/shard_map/ppermute | solution.py:82
  697.9 95.9 %collective-permute-start.153 = (bf16[64,2048]{1,0:T(8,128)(2,1)}, bf16[64,2048]{1,0:T(8,128)(2,1)}, u32[]{:S(2)}, u32[]{:S(2)}) collective-permute-start(bf16[64,2048]{1,0:T(8,128)(2,1)} %get-tuple-element.198), channel_id=1, source_target_pairs={{0,12},{1,13},{2,14},{3,15},{4,0},{5,1},{6,2},{7,3},{8,4},{9,5},{1... | collective-permute-start | bytes 786440 | tf_op jit(solution)/shard_map/ppermute | solution.py:82
  702.0 92.7 %collective-permute-start.157 = (bf16[64,2048]{1,0:T(8,128)(2,1)}, bf16[64,2048]{1,0:T(8,128)(2,1)}, u32[]{:S(2)}, u32[]{:S(2)}) collective-permute-start(bf16[64,2048]{1,0:T(8,128)(2,1)} %get-tuple-element.197), channel_id=1, source_target_pairs={{0,4},{1,5},{2,6},{3,7},{4,8},{5,9},{6,10},{7,11},{8,12},{9,13},{1... | collective-permute-start | bytes 786440 | tf_op jit(solution)/shard_map/ppermute | solution.py:82
  847.8 49.5 %collective-permute-start.286 = (bf16[16,64,352]{2,1,0:T(8,128)(2,1)}, bf16[16,64,352]{2,1,0:T(8,128)(2,1)}, u32[]{:S(2)}, u32[]{:S(2)}) collective-permute-start(bf16[16,64,352]{2,1,0:T(8,128)(2,1)} %dynamic-slice_convert_fusion), channel_id=1, source_target_pairs={{0,16},{16,0},{1,17},{17,1},{2,18},{18,2},{3,19},{19,3},{4,20},{20... | collective-permute-start | bytes 2162696 | tf_op jit(solution)/shard_map/ppermute | solution.py:153
  930.1 39.8 %collective-permute-start.267 = (bf16[16,16,256]{2,1,0:T(8,128)(2,1)}, bf16[16,16,256]{2,1,0:T(8,128)(2,1)}, u32[]{:S(2)}, u32[]{:S(2)}) collective-permute-start(bf16[16,16,256]{2,1,0:T(8,128)(2,1)} %dynamic-slice_convert_fusion.2), channel_id=1, source_target_pairs={{0,16},{16,0},{1,17},{17,1},{2,18},{18,2},{3,19},{19,3},{4,20},{20... | collective-permute-start | bytes 393224 | tf_op jit(solution)/shard_map/ppermute | solution.py:153
  973.0 96.1 %all-to-all-start.10 = ((bf16[16,16,256]{2,1,0:T(8,128)(2,1)}), bf16[16,16,256]{2,1,0:T(8,128)(2,1)}, u32[]{:S(2)}, u32[]{:S(2)}) async-start(bf16[16,16,256]{2,1,0:T(8,128)(2,1)} %add_convert_fusion.75), calls=%async_computation.10 | async-start | bytes 262144 | tf_op jit(solution)/shard_map/all_to_all | solution.py:199
  1005.7 70.8 %collective-permute-start.249 = (bf16[16,64,192]{2,1,0:T(8,128)(2,1)}, bf16[16,64,192]{2,1,0:T(8,128)(2,1)}, u32[]{:S(2)}, u32[]{:S(2)}) collective-permute-start(bf16[16,64,192]{2,1,0:T(8,128)(2,1)} %dynamic-slice_convert_fusion.1), channel_id=1, source_target_pairs={{0,16},{16,0},{1,17},{17,1},{2,18},{18,2},{3,19},{19,3},{4,20},{20... | collective-permute-start | bytes 1179656 | tf_op jit(solution)/shard_map/ppermute | solution.py:153
  1029.5 74.8 %collective-permute-start.223 = (bf16[64,2048]{1,0:T(8,128)(2,1)}, bf16[64,2048]{1,0:T(8,128)(2,1)}, u32[]{:S(2)}, u32[]{:S(2)}) collective-permute-start(bf16[64,2048]{1,0:T(8,128)(2,1)} %get-tuple-element.204), channel_id=1, source_target_pairs={{0,2},{1,3},{2,0},{3,1},{4,6},{5,7},{6,4},{7,5},{8,10},{9,11},{10,... | collective-permute-start | bytes 786440 | tf_op jit(solution)/shard_map/ppermute | solution.py:82
  1031.0 73.4 %collective-permute-start.225 = (bf16[64,2048]{1,0:T(8,128)(2,1)}, bf16[64,2048]{1,0:T(8,128)(2,1)}, u32[]{:S(2)}, u32[]{:S(2)}) collective-permute-start(bf16[64,2048]{1,0:T(8,128)(2,1)} %get-tuple-element.203), channel_id=1, source_target_pairs={{0,1},{1,0},{2,3},{3,2},{4,5},{5,4},{6,7},{7,6},{8,9},{9,8},{10,11... | collective-permute-start | bytes 786440 | tf_op jit(solution)/shard_map/ppermute | solution.py:82
  1034.8 76.3 %collective-permute-start.231 = (bf16[64,2048]{1,0:T(8,128)(2,1)}, bf16[64,2048]{1,0:T(8,128)(2,1)}, u32[]{:S(2)}, u32[]{:S(2)}) collective-permute-start(bf16[64,2048]{1,0:T(8,128)(2,1)} %get-tuple-element.200), channel_id=1, source_target_pairs={{0,2},{1,3},{2,0},{3,1},{4,6},{5,7},{6,4},{7,5},{8,10},{9,11},{10,... | collective-permute-start | bytes 786440 | tf_op jit(solution)/shard_map/ppermute | solution.py:82
  1069.1 174.4 %all-to-all-start.11 = ((bf16[16,64,352]{2,1,0:T(8,128)(2,1)}), bf16[16,64,352]{2,1,0:T(8,128)(2,1)}, u32[]{:S(2)}, u32[]{:S(2)}) async-start(bf16[16,64,352]{2,1,0:T(8,128)(2,1)} %add_convert_fusion.5), calls=%async_computation.11 | async-start | bytes 1572864 | tf_op jit(solution)/shard_map/all_to_all | solution.py:199
  1124.9 41.0 %collective-permute-start.218 = (bf16[64,2048]{1,0:T(8,128)(2,1)}, bf16[64,2048]{1,0:T(8,128)(2,1)}, u32[]{:S(2)}, u32[]{:S(2)}) collective-permute-start(bf16[64,2048]{1,0:T(8,128)(2,1)} %get-tuple-element.199), channel_id=1, source_target_pairs={{0,1},{1,0},{2,3},{3,2},{4,5},{5,4},{6,7},{7,6},{8,9},{9,8},{10,11... | collective-permute-start | bytes 786440 | tf_op jit(solution)/shard_map/ppermute | solution.py:82
  1126.1 41.2 %collective-permute-start.158 = (bf16[64,2048]{1,0:T(8,128)(2,1)}, bf16[64,2048]{1,0:T(8,128)(2,1)}, u32[]{:S(2)}, u32[]{:S(2)}) collective-permute-start(bf16[64,2048]{1,0:T(8,128)(2,1)} %get-tuple-element.169), channel_id=1, source_target_pairs={{0,1},{1,0},{2,3},{3,2},{4,5},{5,4},{6,7},{7,6},{8,9},{9,8},{10,11... | collective-permute-start | bytes 786440 | tf_op jit(solution)/shard_map/ppermute | solution.py:82
  1130.5 37.4 %collective-permute-start.220 = (bf16[64,2048]{1,0:T(8,128)(2,1)}, bf16[64,2048]{1,0:T(8,128)(2,1)}, u32[]{:S(2)}, u32[]{:S(2)}) collective-permute-start(bf16[64,2048]{1,0:T(8,128)(2,1)} %get-tuple-element.207), channel_id=1, source_target_pairs={{0,2},{1,3},{2,0},{3,1},{4,6},{5,7},{6,4},{7,5},{8,10},{9,11},{10,... | collective-permute-start | bytes 786440 | tf_op jit(solution)/shard_map/ppermute | solution.py:82
  1132.5 35.5 %collective-permute-start.160 = (bf16[64,2048]{1,0:T(8,128)(2,1)}, bf16[64,2048]{1,0:T(8,128)(2,1)}, u32[]{:S(2)}, u32[]{:S(2)}) collective-permute-start(bf16[64,2048]{1,0:T(8,128)(2,1)} %get-tuple-element.177), channel_id=1, source_target_pairs={{0,2},{1,3},{2,0},{3,1},{4,6},{5,7},{6,4},{7,5},{8,10},{9,11},{10,... | collective-permute-start | bytes 786440 | tf_op jit(solution)/shard_map/ppermute | solution.py:82
  1180.9 35.2 %collective-permute-start.68 = (bf16[64,2048]{1,0:T(8,128)(2,1)}, bf16[64,2048]{1,0:T(8,128)(2,1)S(1)}, u32[]{:S(2)}, u32[]{:S(2)}) collective-permute-start(bf16[64,2048]{1,0:T(8,128)(2,1)} %get-tuple-element.229), channel_id=1, source_target_pairs={{0,1},{1,0},{2,3},{3,2},{4,5},{5,4},{6,7},{7,6},{8,9},{9,8},{10,11... | collective-permute-start | bytes 786440 | tf_op jit(solution)/shard_map/ppermute | solution.py:82
  1180.9 35.5 %collective-permute-start.70 = (bf16[64,2048]{1,0:T(8,128)(2,1)}, bf16[64,2048]{1,0:T(8,128)(2,1)S(1)}, u32[]{:S(2)}, u32[]{:S(2)}) collective-permute-start(bf16[64,2048]{1,0:T(8,128)(2,1)} %get-tuple-element.237), channel_id=1, source_target_pairs={{0,2},{1,3},{2,0},{3,1},{4,6},{5,7},{6,4},{7,5},{8,10},{9,11},{10,... | collective-permute-start | bytes 786440 | tf_op jit(solution)/shard_map/ppermute | solution.py:82
  1229.3 66.9 %collective-permute-start.269 = (bf16[2048,1024]{1,0:T(8,128)(2,1)}, bf16[2048,1024]{1,0:T(8,128)(2,1)}, u32[]{:S(2)}, u32[]{:S(2)}) collective-permute-start(bf16[2048,1024]{1,0:T(8,128)(2,1)} %convolution_convert_fusion), channel_id=1, source_target_pairs={{0,16},{16,0},{1,17},{17,1},{2,18},{18,2},{3,19},{19,3},{4,20},{20... | collective-permute-start | bytes 12582920 | tf_op jit(solution)/shard_map/ppermute | solution.py:153
  1234.1 86.9 %collective-permute-start.291 = (bf16[704,2048]{1,0:T(8,128)(2,1)}, bf16[704,2048]{1,0:T(8,128)(2,1)}, u32[]{:S(2)}, u32[]{:S(2)}) collective-permute-start(bf16[704,2048]{1,0:T(8,128)(2,1)} %convolution_convert_fusion.1), channel_id=1, source_target_pairs={{0,16},{16,0},{1,17},{17,1},{2,18},{18,2},{3,19},{19,3},{4,20},{20... | collective-permute-start | bytes 8650760 | tf_op jit(solution)/shard_map/ppermute | solution.py:153
  1234.4 112.5 %collective-permute-start.290 = (bf16[704,2048]{1,0:T(8,128)(2,1)}, bf16[704,2048]{1,0:T(8,128)(2,1)}, u32[]{:S(2)}, u32[]{:S(2)}) collective-permute-start(bf16[704,2048]{1,0:T(8,128)(2,1)} %convolution_convert_fusion.2), channel_id=1, source_target_pairs={{0,16},{16,0},{1,17},{17,1},{2,18},{18,2},{3,19},{19,3},{4,20},{20... | collective-permute-start | bytes 8650760 | tf_op jit(solution)/shard_map/ppermute | solution.py:153
  1321.0 45.1 %collective-permute-start.289 = (bf16[704,2048]{1,0:T(8,128)(2,1)}, bf16[704,2048]{1,0:T(8,128)(2,1)S(1)}, u32[]{:S(2)}, u32[]{:S(2)}) collective-permute-start(bf16[704,2048]{1,0:T(8,128)(2,1)} %convolution_convert_fusion.3), channel_id=1, source_target_pairs={{0,16},{16,0},{1,17},{17,1},{2,18},{18,2},{3,19},{19,3},{4,20},{20... | collective-permute-start | bytes 8650760 | tf_op jit(solution)/shard_map/ppermute | solution.py:153
  (478 other events, 9544.0 us)
